TPU v7x, 32 devices: a whole 2x2x4 slice. The times are simulated.
32 devices in a mesh: sfc: 8 (over y, x, core), grp: 4 (over z).
Axes of the slice: x: 2, y: 2, z: 4, core: 2. Of those that a mesh axis runs over, the one named last changes fastest.
Arguments:
- bin_points: float32 [32768, 5, 256], P(('sfc', 'grp')), may hold values from -1 to 1, as said below
- bin_plan: int32 [32768, 1], P(('sfc', 'grp')), may hold values from 0 to 7; in each aligned block of 1024 rows (0 to 1023, 1024 to 2047, ...) at most 128 rows name the same one
- bin_leaf: int32 [32768], P(('sfc', 'grp')), may hold values from 0 to 255
- leaf_slots: int32 [8, 8, 128], P('sfc', None, 'grp'), may hold values from 0 to 127, each once within a row
- box_slots: int32 [8, 8, 16], P('sfc'), may hold values from 0 to 15, each once within a row
- parent_cone: int32 [8, 128], P('sfc'), may hold values from 0 to 15
- box_cone: int32 [8, 16], P('sfc'), may hold values from 0 to 15
- cone_angles: float32 [16, 2], replicated, may hold values from -3.140625 to 3.140625
Outputs:
- leaf_expansions: float32 [8192, 2, 512], P(('sfc', 'grp'))
- level_one: float32 [1024, 2, 512], P(('sfc', 'grp'))
- level_two: float32 [128, 2, 512], P(('sfc', 'grp'))
Inputs may be any that keep to these rules, and one draw needn't show every extreme that they name: `bin_plan`: among the rows of one device no value is named by more than 128 rows, a bound that some block reaches. Each row leaf_slots[s, o, :] names every level-one box of segment s once, so every level-one box has exactly one child of each octant. Each row box_slots[s, o, :] names every level-two box of segment s once. `bin_points`: coordinates lie within -1 to 1 and densities within -0.4 to 0.4.
All inputs are finite; a program needn't handle non-finite values.
Results may differ from a plain program's by a relative error of at most 0.0039.
Values sent between devices are 32-bit elements; how exact they have to be, the bound alone decides.
A program may use at most 320 MiB of HBM per device.

v0:
```python
import functools

import jax
import jax.numpy as jnp
import ml_dtypes
import numpy as np
from jax import lax
from jax.experimental import pallas as pl
from jax.experimental.pallas import tpu as pltpu
from jax.sharding import PartitionSpec as P

kappa_leaf = 2.0
kappa_box = 4.0


def cheb_nodes():
    return np.cos((2.0 * np.arange(8) + 1.0) * np.pi / 16.0)


def lagrange_np(values):
    nodes = cheb_nodes()
    rows = []
    for center in range(8):
        weight = np.ones_like(values)
        for other in range(8):
            if other != center:
                weight = weight * (values - nodes[other]) / (nodes[center] - nodes[other])
        rows.append(weight)
    return np.stack(rows, axis=-2)


def child_axes(octant):
    bits = [octant // 4, octant // 2 % 2, octant % 2]
    nodes = cheb_nodes()
    return np.stack([0.5 * (2 * bit - 1) + 0.5 * nodes for bit in bits])


def child_matrices():
    rows = []
    for octant in range(8):
        first, second, third = [lagrange_np(axis) for axis in child_axes(octant)]
        rows.append(np.einsum("ad,be,cf->abcdef", first, second, third).reshape(512, 512))
    return np.stack(rows)


def basis_constants(width):
    nodes = cheb_nodes()
    rows = np.zeros((5, 8, width))
    for center in range(8):
        pair = min(center, 7 - center)
        others = [nodes[j] ** 2 for j in range(4) if j != pair]
        scale = 2.0 * nodes[center]
        for value in others:
            scale = scale * (nodes[center] ** 2 - value)
        for j in range(3):
            rows[j, center] = others[j]
        rows[3, center] = 1.0 / scale
        rows[4, center] = nodes[center] / scale
    return rows.astype(np.float32)


def octant_tables():
    positions = np.stack([child_axes(octant) for octant in range(8)])
    shape = (8, 8, 8, 8)
    grid = np.stack(
        [
            np.broadcast_to(positions[:, 0][:, :, None, None], shape),
            np.broadcast_to(positions[:, 1][:, None, :, None], shape),
            np.broadcast_to(positions[:, 2][:, None, None, :], shape),
        ],
        axis=1,
    )
    return grid.reshape(8, 3, 512).astype(np.float32)


def node_table():
    nodes = cheb_nodes()
    shape = (8, 8, 8)
    grid = np.stack(
        [
            np.broadcast_to(nodes[:, None, None], shape),
            np.broadcast_to(nodes[None, :, None], shape),
            np.broadcast_to(nodes[None, None, :], shape),
        ]
    )
    return grid.reshape(3, 512).astype(np.float32)


def term_kernel(block, unroll, index_ref, const_ref, point_ref, out_ref):
    step = pl.program_id(0)
    width = point_ref.shape[2]

    @pl.when(step == 0)
    def _():
        def clear(i, carry):
            out_ref[pl.ds(pl.multiple_of(i * 8, 8), 8)] = jnp.zeros((8, 8, 128), jnp.float32)
            return carry

        lax.fori_loop(0, out_ref.shape[0] // 8, clear, 0)

    tau = [const_ref[j] for j in range(5)]
    low = lax.broadcasted_iota(jnp.int32, (8, 128), 1) < 64

    def basis(row):
        row = jnp.broadcast_to(row, (8, width))
        square = row * row
        value = (square - tau[0]) * (square - tau[1]) * (square - tau[2])
        return value * (row * tau[3] + tau[4])

    def factors(i):
        first = basis(point_ref[i, 0:1, :])
        second = basis(point_ref[i, 1:2, :])
        third = basis(point_ref[i, 2:3, :])
        weighted = jnp.concatenate(
            [point_ref[i, 3:4, :] * first, point_ref[i, 4:5, :] * first], axis=0
        ).astype(jnp.bfloat16)
        pair = jnp.concatenate(
            [second[b : b + 1, :] * third for b in range(8)], axis=0
        ).astype(jnp.bfloat16)
        return weighted, pair

    def body(j, carry):
        values = []
        for k in range(unroll):
            i = j * 2 * unroll + 2 * k
            wa, pa = factors(i)
            wb, pb = factors(i + 1)
            result = lax.dot_general(
                jnp.concatenate([wa, wb], axis=0),
                jnp.concatenate([pa, pb], axis=0),
                (((1,), (1,)), ((), ())),
                preferred_element_type=jnp.float32,
            )
            one = jnp.where(low, result[0:8], pltpu.roll(result[8:16], 64, 1))
            two = jnp.where(low, pltpu.roll(result[16:24], 64, 1), result[24:32])
            values.append((i, one))
            values.append((i + 1, two))
        for i, value in values:
            spot = index_ref[step * block + i]
            out_ref[spot] += value
        return carry

    lax.fori_loop(0, block // (2 * unroll), body, 0)


def dense_terms(points, index, rows):
    count, _, width = points.shape
    block = 64
    return pl.pallas_call(
        functools.partial(term_kernel, block, 4),
        out_shape=jax.ShapeDtypeStruct((rows, 8, 128), jnp.float32),
        grid_spec=pltpu.PrefetchScalarGridSpec(
            num_scalar_prefetch=1,
            grid=(count // block,),
            in_specs=[
                pl.BlockSpec((5, 8, width), lambda i, index: (0, 0, 0)),
                pl.BlockSpec((block, 5, width), lambda i, index: (i, 0, 0)),
            ],
            out_specs=pl.BlockSpec((rows, 8, 128), lambda i, index: (0, 0, 0)),
        ),
        compiler_params=pltpu.CompilerParams(vmem_limit_bytes=48 * 1024 * 1024),
        name="bin_terms",
    )(index, jnp.asarray(basis_constants(width)), points)


def rotate(field, cosine, sine):
    real_part = field[:, 0]
    imag_part = field[:, 1]
    return jnp.stack(
        [real_part * cosine - imag_part * sine, real_part * sine + imag_part * cosine], axis=1
    )


def cone_vectors(cone_angles):
    azimuth = cone_angles[:, 0]
    polar = cone_angles[:, 1]
    return jnp.stack(
        [jnp.cos(azimuth) * jnp.sin(polar), jnp.sin(azimuth) * jnp.sin(polar), jnp.cos(polar)],
        axis=1,
    )


def look_up(table, index):
    onehot = (index[:, None] == jnp.arange(table.shape[0], dtype=jnp.int32)[None, :]).astype(
        jnp.float32
    )
    return jnp.dot(
        onehot, table, preferred_element_type=jnp.float32, precision=lax.Precision.HIGHEST
    )


def parent_turn(field, dirs, kappa):
    grid = jnp.asarray(node_table())
    angle = -kappa * (
        dirs[:, 0, None] * grid[0] + dirs[:, 1, None] * grid[1] + dirs[:, 2, None] * grid[2]
    )
    return rotate(field, jnp.cos(angle), jnp.sin(angle))


def split(values):
    high = values.astype(jnp.bfloat16)
    return high, (values - high.astype(jnp.float32)).astype(jnp.bfloat16)


def level_partial(children, slots, parent_dirs, kappa, matrices):
    count = children.shape[0]
    owners = parent_dirs.shape[0]
    parents = jnp.transpose(slots).reshape(count)
    match = jnp.arange(owners, dtype=jnp.int32)[:, None] == parents[None, :]
    child_dirs = jnp.dot(
        jnp.transpose(match.astype(jnp.float32)),
        parent_dirs,
        preferred_element_type=jnp.float32,
        precision=lax.Precision.HIGHEST,
    )
    grid = jnp.asarray(octant_tables())
    grouped = child_dirs.reshape(count // 8, 8, 3)
    angle = (
        grouped[:, :, 0, None] * grid[None, :, 0]
        + grouped[:, :, 1, None] * grid[None, :, 1]
        + grouped[:, :, 2, None] * grid[None, :, 2]
    )
    angle = kappa * angle.reshape(count, 512)
    turned = rotate(children, jnp.cos(angle), jnp.sin(angle))
    moved = jnp.einsum(
        "jopn,omn->jopm",
        turned.reshape(count // 8, 8, 2, 512).astype(jnp.bfloat16),
        matrices,
        preferred_element_type=jnp.float32,
    )
    picks = match.astype(jnp.bfloat16)
    high, low = split(moved.reshape(count, 1024))
    total = jnp.dot(picks, high, preferred_element_type=jnp.float32) + jnp.dot(
        picks, low, preferred_element_type=jnp.float32
    )
    return total.reshape(owners, 2, 512)


def per_device(
    bin_points, bin_plan, bin_leaf, leaf_slots, box_slots, parent_cone, box_cone, cone_angles
):
    peers = lax.axis_size("sfc")
    groups = lax.axis_size("grp")
    group_rank = lax.axis_index("grp")
    leaf_count = leaf_slots.shape[2] * 8
    index = bin_plan[:, 0] * leaf_count + bin_leaf
    dense = dense_terms(bin_points, index, peers * leaf_count)
    own = lax.psum_scatter(dense, "sfc", scatter_dimension=0, tiled=True)
    leaves = jnp.transpose(own.reshape(leaf_count, 8, 2, 64), (0, 2, 1, 3)).reshape(
        leaf_count, 2, 512
    )
    matrices = jnp.asarray(child_matrices().astype(ml_dtypes.bfloat16))
    directions = cone_vectors(cone_angles)
    parent_dirs = look_up(directions, parent_cone[0])
    upper_dirs = look_up(directions, box_cone[0])
    first_owned = parent_dirs.shape[0] // groups
    second_owned = upper_dirs.shape[0] // groups
    partial_value = level_partial(leaves, leaf_slots[0], parent_dirs, kappa_leaf, matrices)
    summed = lax.psum_scatter(partial_value, "grp", scatter_dimension=0, tiled=True)
    mine = lax.dynamic_slice_in_dim(parent_dirs, group_rank * first_owned, first_owned, 0)
    first_level = parent_turn(summed, mine, kappa_leaf)
    slots_mine = lax.dynamic_slice_in_dim(
        box_slots[0], group_rank * (first_owned // 8), first_owned // 8, 1
    )
    upper = level_partial(first_level, slots_mine, upper_dirs, kappa_box, matrices)
    upper_owned = lax.psum_scatter(upper, "grp", scatter_dimension=0, tiled=True)
    upper_mine = lax.dynamic_slice_in_dim(upper_dirs, group_rank * second_owned, second_owned, 0)
    second_level = parent_turn(upper_owned, upper_mine, kappa_box)
    return (leaves, first_level, second_level)


def solution(mesh):
    placed = (
        P(("sfc", "grp"), None, None),
        P(("sfc", "grp"), None),
        P(("sfc", "grp")),
        P("sfc", None, "grp"),
        P("sfc", None, None),
        P("sfc", None),
        P("sfc", None),
        P(),
    )
    return jax.shard_map(
        per_device,
        mesh=mesh,
        in_specs=placed,
        out_specs=(
            P(("sfc", "grp"), None, None),
            P(("sfc", "grp"), None, None),
            P(("sfc", "grp"), None, None),
        ),
        check_vma=False,
    )
```

profile of v0, /device:TPU:0, one launch (start us, length us, event | category | flops | bytes accessed | tf_op | source)
XLA Modules:
  0.0 213.8 jit_solution(1918093902728360311)
XLA Ops:
  7.2 0.0 reduce-scatter.3.cloned.1.call-start
  7.2 0.7 broadcast_multiply_fusion
  7.9 9.0 %copy.58.point_ref = f32[1024,5,256]{2,1,0:T(8,128)} copy(f32[1024,5,256]{2,0,1:T(8,128)} %param.14) | data formatting | bytes 10485760 | tf_op args[0]
  16.9 44.0 %bin_terms.1 = f32[2048,8,128]{2,1,0:T(8,128)} custom-call(s32[1024]{0:T(1024)S(1)} %add.160.index_ref, f32[5,8,256]{2,1,0:T(8,128)S(1)} %copy-done.1, f32[1024,5,256]{2,1,0:T(8,128)} %copy.58.point_ref), custom_call_target="tpu_custom_call" | custom-call | tf_op jit(solution)/shard_map/bin_terms/pallas_call | solution.py:149
  61.0 0.0 reduce-scatter.3.cloned.1.call-update
  61.0 0.0 reduce-scatter.5.cloned.1.call-start
  61.1 0.1 constant_dynamic-slice_fusion.1
  61.1 0.1 copy.71
  61.2 0.1 eq.69
  61.3 0.3 copy-done.2
  61.7 0.2 copy.64
  61.9 0.1 copy.61
  62.0 0.1 eq.61
  62.1 0.1 cosine_multiply_fusion
  62.2 0.2 fusion.24
  62.3 0.2 fusion.4
  62.5 0.1 reshape.1221
  62.7 0.1 mul.519
  62.8 0.1 broadcast_bitcast_fusion.1
  62.8 0.2 copy.63
  63.1 0.1 mul.513
  63.1 0.1 broadcast_bitcast_fusion.2
  63.2 0.2 copy.62
  63.4 0.1 mul.507
  63.5 0.2 fusion.32
  63.7 1.8 fusion.43
  65.5 69.6 %reduce-scatter.3.cloned.1.call-done = f32[256,8,128]{2,1,0:T(8,128)} async-done(((f32[2048,8,128]{2,1,0:T(8,128)}), f32[256,8,128]{2,1,0:T(8,128)}) %reduce-scatter.3.cloned.1.call-update) | async-done | bytes 1048592 | tf_op jit(solution)/shard_map/reduce_scatter | solution.py:248
  135.1 1.6 copy.59
  136.7 0.1 copy.60
  136.8 1.8 subtract_convert_fusion.2
  138.7 0.1 copy.66
  138.8 0.1 copy.68
  138.9 0.1 copy.65
  139.0 0.1 copy.67
  139.1 3.6 %convolution_bitcast_fusion = f32[32,8,2,512]{3,0,2,1:T(8,128)S(1)} fusion(bf16[8,512,512,1]{2,1,3,0:T(8,128)(2,1)} %constant.57, bf16[32,8,1,512]{3,0,2,1:T(8,128)(2,1)S(1)} %copy.68, bf16[32,8,1,512]{3,0,2,1:T(8,128)(2,1)S(1)} %copy.67), kind=kOutput, calls=%fused_computation | convolution fusion | flops 268697600 | bytes 5767168 | tf_op jit(solution)/shard_map/jopn,omn->jopm/dot_general | solution.py:225
  142.7 0.8 copy.93
  143.5 0.2 copy.84
  143.8 0.2 fusion.2
  144.0 0.2 convolution_add_fusion
  144.2 0.8 copy.94
  145.1 0.0 reduce-scatter.5.cloned.1.call-update
  145.1 0.2 all-reduce.3.cloned.1.call-start
  145.4 0.1 fusion.31
  145.5 0.1 reshape.1224
  145.6 0.1 mul.560
  145.7 0.1 mul.554
  145.7 0.1 mul.548
  145.8 0.6 dynamic-slice.1
  147.1 0.1 constant_dynamic-slice_fusion
  147.1 0.1 constant_dynamic-slice_fusion.2
  147.2 1.3 copy.77
  148.5 18.4 %reduce-scatter.5.cloned.1.call-done = f32[32,2,512]{2,0,1:T(8,128)} async-done(((f32[128,2,512]{2,0,1:T(8,128)}), f32[32,2,512]{2,0,1:T(8,128)}) %reduce-scatter.5.cloned.1.call-update) | async-done | bytes 131088 | tf_op jit(solution)/shard_map/reduce_scatter | solution.py:259
  166.9 1.5 fusion.30
  168.4 0.3 fusion.29
  168.8 3.4 %convolution_bitcast_fusion.1 = f32[4,8,2,512]{3,0,2,1:T(4,128)S(1)} fusion(bf16[8,512,512,1]{2,1,3,0:T(8,128)(2,1)} %constant.57, bf16[4,8,1,512]{3,0,2,1:T(4,128)(2,1)S(1)} %copy.73, bf16[4,8,1,512]{3,0,2,1:T(4,128)(2,1)S(1)} %copy.72), kind=kOutput, calls=%fused_computation.2 | convolution fusion | flops 33685504 | bytes 4390912 | tf_op jit(solution)/shard_map/jopn,omn->jopm/dot_general | solution.py:225
  172.2 0.1 copy.95
  172.3 0.1 fusion.26
  172.4 0.1 convolution_add_fusion.1
  172.5 0.7 reshape.1226
  173.3 0.8 copy.78
  174.0 31.6 %all-reduce.3.cloned.1.call-done = f32[16,2,512]{2,1,0:T(2,128)} async-done(((f32[16,2,512]{2,1,0:T(2,128)}), f32[16,2,512]{2,1,0:T(2,128)}) %all-reduce.3.cloned.1.call-update) | async-done | bytes 65552
  205.7 0.8 constant_dynamic-slice_fusion.3
  206.5 0.2 multiply_subtract_fusion.1
  206.6 0.6 copy.79
  (39 shorter events, 0.2 us)
Async XLA Ops:
  7.2 53.9 %copy-start = (s32[1,8,16]{2,1,0:T(8,128)S(1)}, s32[1,8,16]{2,1,0:T(8,128)}, u32[]{:S(2)}) copy-start(s32[1,8,16]{2,1,0:T(8,128)} %param.18) | copy-start | bytes 1540
  7.2 128.0 %reduce-scatter.3.cloned.1.call-start = ((), (), s32[]{:S(2)}) async-start(), calls=%async_computation.2 | async-start | bytes 9437184 | tf_op jit(solution)/shard_map/reduce_scatter | solution.py:248
  7.9 9.0 %copy-start.8 = (s32[1024]{0:T(1024)S(1)}, s32[1024]{0:T(1024)}, u32[]{:S(2)}) copy-start(s32[1024]{0:T(1024)} %param.16) | copy-start | bytes 12292
  7.9 9.0 %copy-start.1 = (f32[5,8,256]{2,1,0:T(8,128)S(1)}, f32[5,8,256]{2,1,0:T(8,128)}, u32[]{:S(2)}) copy-start(f32[5,8,256]{2,1,0:T(8,128)} %constant.33.clone.const_ref) | copy-start | bytes 122884
  60.9 0.7 copy-start.2
  60.9 1.0 copy-start.9
  60.9 1.2 copy-start.10
  60.9 1.2 copy-start.11
  60.9 1.8 copy-start.3
  61.0 2.2 %copy-start.4 = (f32[8,512]{1,0:T(8,128)S(1)}, f32[8,512]{1,0:T(8,128)}, u32[]{:S(2)}) copy-start(f32[8,512]{1,0:T(8,128)} %constant.42) | copy-start | bytes 49156
  61.0 2.5 %copy-start.12 = (s32[1,16]{1,0:T(1,128)S(1)}, s32[1,16]{1,0:T(1,128)}, u32[]{:S(2)}) copy-start(s32[1,16]{1,0:T(1,128)} %param.20) | copy-start | bytes 196
  61.0 105.9 %reduce-scatter.5.cloned.1.call-start = ((), (), s32[]{:S(2)}) async-start(), calls=%async_computation.3 | async-start | bytes 655360 | tf_op jit(solution)/shard_map/reduce_scatter | solution.py:259
  143.5 2.3 %copy-start.13 = (u32[32]{0:T(128)S(1)}, u32[32]{0:T(128)}, u32[]{:S(2)}) copy-start(u32[32]{0:T(128)} %constant.55) | copy-start | bytes 388
  143.7 23.2 %copy-start.5 = (f32[512]{0:T(512)S(1)}, f32[512]{0:T(512)}, u32[]{:S(2)}) copy-start(f32[512]{0:T(512)} %constant.52) | copy-start | bytes 6148
  143.7 23.1 %copy-start.6 = (f32[512]{0:T(512)S(1)}, f32[512]{0:T(512)}, u32[]{:S(2)}) copy-start(f32[512]{0:T(512)} %constant.50) | copy-start | bytes 6148
  143.8 23.1 %copy-start.7 = (f32[512]{0:T(512)S(1)}, f32[512]{0:T(512)}, u32[]{:S(2)}) copy-start(f32[512]{0:T(512)} %constant.48) | copy-start | bytes 6148
  145.1 60.5 %all-reduce.3.cloned.1.call-start = ((), (), s32[]{:S(2)}) async-start(), calls=%async_computation.4 | async-start | bytes 131072
Sparse Core Ops, SparseCore 0:
  61.1 73.9 reduce-scatter.2
  145.2 21.5 reduce-scatter.4
  173.4 32.2 all-reduce.2
where the time goes:
time: 214 us
  waiting for transfers between devices  120 us (56%)
  Pallas kernels  44 us (21%)
  local copies, waits for them, and re-layouts  20.3 us (9%)
  between operations  14.8 us (7%)
  matrix products  8.39 us (4%)
  other arithmetic  6.38 us (3%)
    reduce_scatter x1, waiting for transfers between devices, per_device(): own = lax.psum_scatter(dense, 'sfc', scatter_dimension=0, tiled=True)  69.6 us
    pallas_call x1, Pallas kernels, dense_terms(): pl.pallas_call(functools.partial(term_kernel, block, 4), out_shape=jax.Sh...  44 us
    unnamed x4, waiting for transfers between devices  31.7 us
    reduce_scatter x1, waiting for transfers between devices, per_device(): lax.psum_scatter(partial_value, 'grp', scatter_dimension=0, tiled=True)  18.4 us
    unnamed x35, local copies, waits for them, and re-layouts  12.9 us
    dot_general x2, matrix products, level_partial(): jnp.einsum('jopn,omn->jopm', turned.reshape(count // 8, 8, 2, 512).astype...  6.96 us
  transfers between devices with their start and end apart: 3, of which 3 were waited for; matrix products, arithmetic and copies ran while one was open for 3% of the time, Pallas kernels for 0%

commit v1 on v0

--- a/solution.py
+++ b/solution.py
@@ -107,60 +107,229 @@
         value = (square - tau[0]) * (square - tau[1]) * (square - tau[2])
         return value * (row * tau[3] + tau[4])
 
-    def factors(i):
-        first = basis(point_ref[i, 0:1, :])
-        second = basis(point_ref[i, 1:2, :])
-        third = basis(point_ref[i, 2:3, :])
+    def factors(rows, i):
+        first = basis(rows[0, i : i + 1])
+        second = basis(rows[1, i : i + 1])
+        third = basis(rows[2, i : i + 1])
         weighted = jnp.concatenate(
-            [point_ref[i, 3:4, :] * first, point_ref[i, 4:5, :] * first], axis=0
+            [rows[3, i : i + 1] * first, rows[4, i : i + 1] * first], axis=0
         ).astype(jnp.bfloat16)
         pair = jnp.concatenate(
-            [second[b : b + 1, :] * third for b in range(8)], axis=0
+            [second[b : b + 1] * third for b in range(8)], axis=0
         ).astype(jnp.bfloat16)
         return weighted, pair
 
     def body(j, carry):
+        base = pl.multiple_of(j * 2 * unroll, 8)
+        rows = point_ref[:, pl.ds(base, 2 * unroll), :]
         values = []
         for k in range(unroll):
-            i = j * 2 * unroll + 2 * k
-            wa, pa = factors(i)
-            wb, pb = factors(i + 1)
+            wa, pa = factors(rows, 2 * k)
+            wb, pb = factors(rows, 2 * k + 1)
             result = lax.dot_general(
                 jnp.concatenate([wa, wb], axis=0),
                 jnp.concatenate([pa, pb], axis=0),
                 (((1,), (1,)), ((), ())),
                 preferred_element_type=jnp.float32,
             )
-            one = jnp.where(low, result[0:8], pltpu.roll(result[8:16], 64, 1))
-            two = jnp.where(low, pltpu.roll(result[16:24], 64, 1), result[24:32])
-            values.append((i, one))
-            values.append((i + 1, two))
-        for i, value in values:
-            spot = index_ref[step * block + i]
-            out_ref[spot] += value
+            values.append(jnp.where(low, result[0:8], pltpu.roll(result[8:16], 64, 1)))
+            values.append(jnp.where(low, pltpu.roll(result[16:24], 64, 1), result[24:32]))
+        for i, value in enumerate(values):
+            out_ref[index_ref[step * block + base + i]] += value
         return carry
 
     lax.fori_loop(0, block // (2 * unroll), body, 0)
 
 
 def dense_terms(points, index, rows):
-    count, _, width = points.shape
-    block = 64
+    _, count, width = points.shape
+    block = 128
     return pl.pallas_call(
-        functools.partial(term_kernel, block, 4),
+        functools.partial(term_kernel, block, 16),
         out_shape=jax.ShapeDtypeStruct((rows, 8, 128), jnp.float32),
         grid_spec=pltpu.PrefetchScalarGridSpec(
             num_scalar_prefetch=1,
             grid=(count // block,),
             in_specs=[
                 pl.BlockSpec((5, 8, width), lambda i, index: (0, 0, 0)),
-                pl.BlockSpec((block, 5, width), lambda i, index: (i, 0, 0)),
+                pl.BlockSpec((5, block, width), lambda i, index: (0, i, 0)),
             ],
             out_specs=pl.BlockSpec((rows, 8, 128), lambda i, index: (0, 0, 0)),
         ),
         compiler_params=pltpu.CompilerParams(vmem_limit_bytes=48 * 1024 * 1024),
         name="bin_terms",
     )(index, jnp.asarray(basis_constants(width)), points)
+
+
+def greet(axis, targets):
+    barrier = pltpu.get_barrier_semaphore()
+    for target in targets:
+        pl.semaphore_signal(
+            barrier, inc=1, device_id={axis: target}, device_id_type=pl.DeviceIdType.MESH
+        )
+    pl.semaphore_wait(barrier, len(targets))
+
+
+def halving_plan(n):
+    depth = n.bit_length() - 1
+    orders = [[0] + list(range(1, depth)), [0] + list(range(depth - 1, 0, -1))]
+    plans = []
+    for order in orders:
+        stages = []
+        for s, bit in enumerate(order):
+            rest = order[s + 1 :]
+            masks = [
+                m
+                for m in range(n)
+                if (m >> bit) % 2 == 1 and all((m >> k) % 2 == 0 for k in order[:s])
+            ]
+            masks.sort(key=lambda m: tuple(-((m >> k) % 2) for k in rest))
+            stages.append((bit, masks))
+        plans.append(stages)
+    return plans
+
+
+def halving_kernel(axis, n, dense_ref, out_ref, kept, got, load_sem, send_sem, recv_sem):
+    me = lax.axis_index(axis)
+    depth = n.bit_length() - 1
+    half = out_ref.shape[0] // 2
+    bits = [(me // 2**k) % 2 for k in range(depth)]
+    plans = halving_plan(n)
+    partners = [me + 2**k * (1 - 2 * bits[k]) for k in range(depth)]
+    greet(axis, partners)
+
+    def block(mask):
+        return sum(2**k * ((bits[k] + (mask >> k) % 2) % 2) for k in range(depth))
+
+    slots = {}
+    for h in range(2):
+        for s, (bit, masks) in enumerate(plans[h]):
+            for mask in masks:
+                slots[(h, s, mask)] = len(slots)
+    copies = {}
+
+    def send(h, s, mask, source):
+        slot = slots[(h, s, mask)]
+        copy = pltpu.make_async_remote_copy(
+            src_ref=source,
+            dst_ref=got.at[slot],
+            send_sem=send_sem.at[slot],
+            recv_sem=recv_sem.at[slot],
+            device_id={axis: partners[plans[h][s][0]]},
+            device_id_type=pl.DeviceIdType.MESH,
+        )
+        copy.start()
+        copies[(h, s, mask)] = copy
+
+    for j in range(n // 2):
+        for h in range(2):
+            mask = plans[h][0][1][j]
+            send(h, 0, mask, dense_ref.at[block(mask), pl.ds(h * half, half)])
+    loads = {}
+    for j in range(n // 2):
+        for h in range(2):
+            mask = plans[h][0][1][j] - 1
+            load = pltpu.make_async_copy(
+                dense_ref.at[block(mask), pl.ds(h * half, half)],
+                kept.at[h, mask // 2],
+                load_sem.at[h, mask // 2],
+            )
+            load.start()
+            loads[(h, mask)] = load
+    for s in range(depth):
+        for j in range(n >> (s + 1)):
+            for h in range(2):
+                bit, masks = plans[h][s]
+                mask = masks[j]
+                goal = mask - 2**bit
+                if s == 0:
+                    loads[(h, goal)].wait()
+                copies[(h, s, mask)].wait_recv()
+                slot = slots[(h, s, mask)]
+
+                def add(i, carry, h=h, goal=goal, slot=slot):
+                    rows = pl.ds(pl.multiple_of(i * 8, 8), 8)
+                    total = kept[h, goal // 2, rows] + got[slot, rows]
+                    if goal == 0 and s == depth - 1:
+                        out_ref[pl.ds(pl.multiple_of(h * half + i * 8, 8), 8)] = total
+                    else:
+                        kept[h, goal // 2, rows] = total
+                    return carry
+
+                lax.fori_loop(0, half // 8, add, 0)
+                if goal and (goal >> plans[h][s + 1][0]) % 2 == 1:
+                    send(h, s + 1, goal, kept.at[h, goal // 2])
+    for copy in copies.values():
+        copy.wait_send()
+
+
+def halving_scatter(dense, axis, n, number):
+    rows = dense.shape[1]
+    tile = dense.shape[2:]
+    half = rows // 2
+    return pl.pallas_call(
+        functools.partial(halving_kernel, axis, n),
+        out_shape=jax.ShapeDtypeStruct((rows,) + tile, jnp.float32),
+        in_specs=[pl.BlockSpec(memory_space=pl.ANY)],
+        out_specs=pl.BlockSpec(memory_space=pltpu.VMEM),
+        scratch_shapes=[
+            pltpu.VMEM((2, n // 2, half) + tile, jnp.float32),
+            pltpu.VMEM((2 * (n - 1), half) + tile, jnp.float32),
+            pltpu.SemaphoreType.DMA((2, n // 2)),
+            pltpu.SemaphoreType.DMA((2 * (n - 1),)),
+            pltpu.SemaphoreType.DMA((2 * (n - 1),)),
+        ],
+        compiler_params=pltpu.CompilerParams(
+            collective_id=number, has_side_effects=True, vmem_limit_bytes=48 * 1024 * 1024
+        ),
+        name="segment_sums",
+    )(dense)
+
+
+def direct_kernel(axis, n, part_ref, out_ref, got, send_sem, recv_sem):
+    me = lax.axis_index(axis)
+    targets = [lax.rem(me + d, n) for d in range(1, n)]
+    greet(axis, targets)
+    copies = []
+    for d in range(n - 1):
+        copy = pltpu.make_async_remote_copy(
+            src_ref=part_ref.at[targets[d]],
+            dst_ref=got.at[d],
+            send_sem=send_sem.at[d],
+            recv_sem=recv_sem.at[d],
+            device_id={axis: targets[d]},
+            device_id_type=pl.DeviceIdType.MESH,
+        )
+        copy.start()
+        copies.append(copy)
+    total = part_ref[me]
+    for copy in copies:
+        copy.wait_recv()
+    for d in range(n - 1):
+        total = total + got[d]
+    out_ref[...] = total
+    for copy in copies:
+        copy.wait_send()
+
+
+def direct_scatter(parts, axis, n, number):
+    rows = parts.shape[0] // n
+    width = parts.shape[1]
+    return pl.pallas_call(
+        functools.partial(direct_kernel, axis, n),
+        out_shape=jax.ShapeDtypeStruct((rows, width), jnp.float32),
+        in_specs=[pl.BlockSpec(memory_space=pltpu.VMEM)],
+        out_specs=pl.BlockSpec(memory_space=pltpu.VMEM),
+        scratch_shapes=[
+            pltpu.VMEM((n - 1, rows, width), jnp.float32),
+            pltpu.SemaphoreType.DMA((n - 1,)),
+            pltpu.SemaphoreType.DMA((n - 1,)),
+        ],
+        compiler_params=pltpu.CompilerParams(
+            collective_id=number, has_side_effects=True, vmem_limit_bytes=32 * 1024 * 1024
+        ),
+        name="group_sums",
+    )(parts.reshape(n, rows, width))
 
 
 def rotate(field, cosine, sine):
@@ -222,18 +391,19 @@
     )
     angle = kappa * angle.reshape(count, 512)
     turned = rotate(children, jnp.cos(angle), jnp.sin(angle))
-    moved = jnp.einsum(
-        "jopn,omn->jopm",
-        turned.reshape(count // 8, 8, 2, 512).astype(jnp.bfloat16),
-        matrices,
-        preferred_element_type=jnp.float32,
+    moved = sum(
+        jnp.einsum("jopn,omn->jopm", value, matrix, preferred_element_type=jnp.float32)
+        for value, matrix in zip(
+            split(turned.reshape(count // 8, 8, 2, 512)) + split(turned.reshape(count // 8, 8, 2, 512))[:1],
+            (matrices[0], matrices[0], matrices[1]),
+        )
     )
     picks = match.astype(jnp.bfloat16)
     high, low = split(moved.reshape(count, 1024))
     total = jnp.dot(picks, high, preferred_element_type=jnp.float32) + jnp.dot(
         picks, low, preferred_element_type=jnp.float32
     )
-    return total.reshape(owners, 2, 512)
+    return total
 
 
 def per_device(
@@ -244,26 +414,29 @@
     group_rank = lax.axis_index("grp")
     leaf_count = leaf_slots.shape[2] * 8
     index = bin_plan[:, 0] * leaf_count + bin_leaf
-    dense = dense_terms(bin_points, index, peers * leaf_count)
-    own = lax.psum_scatter(dense, "sfc", scatter_dimension=0, tiled=True)
+    dense = dense_terms(jnp.transpose(bin_points, (1, 0, 2)), index, peers * leaf_count)
+    own = halving_scatter(dense.reshape(peers, leaf_count, 8, 128), "sfc", peers, 0)
     leaves = jnp.transpose(own.reshape(leaf_count, 8, 2, 64), (0, 2, 1, 3)).reshape(
         leaf_count, 2, 512
     )
-    matrices = jnp.asarray(child_matrices().astype(ml_dtypes.bfloat16))
+    exact = child_matrices()
+    rounded = exact.astype(ml_dtypes.bfloat16)
+    rest = (exact - rounded.astype(np.float64)).astype(ml_dtypes.bfloat16)
+    matrices = (jnp.asarray(rounded), jnp.asarray(rest))
     directions = cone_vectors(cone_angles)
     parent_dirs = look_up(directions, parent_cone[0])
     upper_dirs = look_up(directions, box_cone[0])
     first_owned = parent_dirs.shape[0] // groups
     second_owned = upper_dirs.shape[0] // groups
     partial_value = level_partial(leaves, leaf_slots[0], parent_dirs, kappa_leaf, matrices)
-    summed = lax.psum_scatter(partial_value, "grp", scatter_dimension=0, tiled=True)
+    summed = direct_scatter(partial_value, "grp", groups, 1).reshape(first_owned, 2, 512)
     mine = lax.dynamic_slice_in_dim(parent_dirs, group_rank * first_owned, first_owned, 0)
     first_level = parent_turn(summed, mine, kappa_leaf)
     slots_mine = lax.dynamic_slice_in_dim(
         box_slots[0], group_rank * (first_owned // 8), first_owned // 8, 1
     )
     upper = level_partial(first_level, slots_mine, upper_dirs, kappa_box, matrices)
-    upper_owned = lax.psum_scatter(upper, "grp", scatter_dimension=0, tiled=True)
+    upper_owned = direct_scatter(upper, "grp", groups, 2).reshape(second_owned, 2, 512)
     upper_mine = lax.dynamic_slice_in_dim(upper_dirs, group_rank * second_owned, second_owned, 0)
     second_level = parent_turn(upper_owned, upper_mine, kappa_box)
     return (leaves, first_level, second_level)

time: 214 us -> 122 us (0.57)
  waiting for transfers between devices: 120 us -> 0 us
  Pallas kernels: 44 us -> 88.6 us
  between operations: 14.8 us -> 1.09 us
  local copies, waits for them, and re-layouts: 20.3 us -> 11.9 us
  matrix products: 8.39 us -> 13.9 us
    reduce_scatter x2 -> x0, waiting for transfers between devices: 88 us -> none  [the longest x1 69.6 us: per_device(): own = lax.psum_scatter(dense, 'sfc', scatter_dimension=0, tiled=True)]
    pallas_call x1 -> x4, Pallas kernels: 44 us -> 88.6 us  [the longest x1 42 us: halving_scatter(): pl.pallas_call(functools.partial(halving_kernel, axis, n), out_shape=jax....]
    unnamed x4 -> x0, waiting for transfers between devices: 31.7 us -> none
    dot_general x2 -> x6, matrix products: 6.96 us -> 12.5 us  [level_partial(): jnp.einsum('jopn,omn->jopm', value, matrix, preferred_element_type=jnp.fl...]
    unnamed x35 -> x41, local copies, waits for them, and re-layouts: 12.9 us -> 7.43 us
  transfers between devices with their start and end apart: 3 -> 0, of which waited for: 3 -> 0; matrix products, arithmetic and copies ran while one was open for 3% -> 0% of each run, Pallas kernels for 0% -> 0%
where the time goes in v1:
time: 122 us
  Pallas kernels  88.6 us (73%)
  matrix products  13.9 us (11%)
  local copies, waits for them, and re-layouts  11.9 us (10%)
  other arithmetic  6.37 us (5%)
    pallas_call x1, Pallas kernels, halving_scatter(): pl.pallas_call(functools.partial(halving_kernel, axis, n), out_shape=jax....  42 us
    pallas_call x1, Pallas kernels, dense_terms(): pl.pallas_call(functools.partial(term_kernel, block, 16), out_shape=jax.S...  25.4 us
    pallas_call x2, Pallas kernels, direct_scatter(): pl.pallas_call(functools.partial(direct_kernel, axis, n), out_shape=jax.S...  21.2 us
    dot_general x6, matrix products, level_partial(): jnp.einsum('jopn,omn->jopm', value, matrix, preferred_element_type=jnp.fl...  12.5 us
    unnamed x41, local copies, waits for them, and re-layouts  7.43 us

profile of v1, /device:TPU:0, one launch (start us, length us, event | category | flops | bytes accessed | tf_op | source)
XLA Modules:
  0.0 121.9 jit_solution(9216812780399022314)
XLA Ops:
  0.6 0.7 broadcast_multiply_fusion
  1.3 0.7 add.174.index_ref
  2.0 2.5 %copy-done.1 = f32[1024,5,256]{2,0,1:T(8,128)S(1)} copy-done((f32[1024,5,256]{2,0,1:T(8,128)S(1)}, f32[1024,5,256]{2,0,1:T(8,128)}, u32[]{:S(2)}) %copy-start.1) | copy-done | bytes 5242904
  4.5 0.8 copy-done.2
  5.3 25.4 %bin_terms.1 = f32[2048,8,128]{2,1,0:T(8,128)} custom-call(s32[1024]{0:T(1024)S(1)} %add.174.index_ref, f32[5,8,256]{2,1,0:T(8,128)S(1)} %copy-done.2, f32[5,1024,256]{2,1,0:T(8,128)S(1)} %bitcast.174), custom_call_target="tpu_custom_call" | custom-call | tf_op jit(solution)/shard_map/bin_terms/pallas_call | solution.py:147
  30.7 42.0 %segment_sums.1 = f32[256,8,128]{2,1,0:T(8,128)S(1)} custom-call(f32[8,256,8,128]{3,2,1,0:T(8,128)} %bitcast.177), custom_call_target="tpu_custom_call" | custom-call | tf_op jit(solution)/shard_map/segment_sums/pallas_call | solution.py:270
  72.8 0.4 copy.39
  73.2 0.1 copy.40
  73.3 1.3 %copy.58 = f32[256,2,512]{2,1,0:T(2,128)} copy(f32[256,2,512]{0,2,1:T(8,128)S(1)} %bitcast.178) | data formatting | bytes 2097152
  74.6 0.1 cosine_multiply_fusion
  74.7 0.2 fusion.30
  74.8 0.1 constant_dynamic-slice_fusion.1
  74.9 0.1 copy.52
  75.0 0.1 eq.69
  75.1 0.1 fusion.29
  75.2 0.1 reshape.1233
  75.3 0.1 mul.560
  75.4 0.1 mul.554
  75.5 0.1 mul.548
  75.6 0.1 broadcast_bitcast_fusion
  75.6 0.2 copy.44
  75.9 0.2 fusion.24
  76.1 0.1 copy.41
  76.1 0.2 eq.61
  76.3 0.1 fusion.5
  76.4 0.1 reshape.1229
  76.6 0.1 mul.519
  76.7 0.1 broadcast_bitcast_fusion.1
  76.7 0.2 copy.43
  76.9 0.1 mul.513
  77.1 0.2 copy.42
  77.3 0.1 mul.507
  77.4 1.8 %fusion.47 = (f32[256,1,512]{0,2,1:T(8,128)S(1)}, f32[256,1,512]{0,2,1:T(8,128)S(1)}) fusion(f32[256,1,512]{0,2,1:T(8,128)S(1)} %copy.44, f32[256]{0:T(256)S(1)} %mul.519, f32[256,1,512]{0,2,1:T(8,128)S(1)} %copy.43, f32[256]{0:T(256)S(1)} %mul.513, f32[256,1,512]{0,2,1:T(8,128)S(1)} %copy.42, f32[256]{0:T(256)S(1)} %mul.507), kind=kLoop, calls=%fused_computation.99 | loop fusion | flops 786432 | bytes 2624512 | tf_op jit(solution)/shard_map/cos | solution.py:393
  79.2 2.0 %multiply_add_fusion = (f32[256,1,512]{0,2,1:T(8,128)S(1)}, f32[256,1,512]{0,2,1:T(8,128)S(1)}) fusion(f32[256,1,512]{0,2,1:T(8,128)S(1)} %get-tuple-element.12, f32[256,2,512]{0,2,1:T(8,128)S(1)} %bitcast.179, f32[256,1,512]{0,2,1:T(8,128)S(1)} %get-tuple-element.13), kind=kLoop, calls=%fused_computation.13 | loop fusion | flops 786432 | bytes 3145728 | tf_op jit(solution)/shard_map/add | solution.py:339
  81.2 0.2 copy.45
  81.4 0.3 copy_dynamic-update-slice_fusion.1
  81.7 0.2 copy.46
  82.0 0.3 copy_dynamic-update-slice_fusion
  82.3 3.7 %fusion.41 = f32[8,32,2,512]{3,1,2,0:T(8,128)S(1)} fusion(bf16[8,512,512,1]{2,1,3,0:T(8,128)(2,1)} %constant.56, f32[32,8,2,512]{3,0,2,1:T(8,128)S(1)} %copy_dynamic-update-slice_fusion), kind=kOutput, calls=%fused_computation.93 | convolution fusion | flops 268697600 | bytes 6291456 | tf_op jit(solution)/shard_map/jopn,omn->jopm/dot_general | solution.py:395
  86.1 1.4 %convolution_add_fusion.1 = f32[8,32,2,512]{3,1,2,0:T(8,128)S(1)} fusion(f32[8,32,2,512]{3,1,2,0:T(8,128)S(1)} %fusion.41, bf16[8,512,512,1]{2,1,3,0:T(8,128)(2,1)S(1)} %copy-done.3, f32[32,8,2,512]{3,0,2,1:T(8,128)S(1)} %copy_dynamic-update-slice_fusion), kind=kOutput, calls=%fused_computation.2 | convolution fusion | flops 269746176 | bytes 7340032 | tf_op jit(solution)/shard_map/jopn,omn->jopm/dot_general | solution.py:395
  87.4 0.8 copy-done.5
  88.2 1.4 %fusion = f32[32,8,2,512]{3,0,2,1:T(8,128)S(1)} fusion(f32[8,32,2,512]{3,1,2,0:T(8,128)S(1)} %convolution_add_fusion.1, bf16[8,512,512,1]{2,1,3,0:T(8,128)(2,1)S(1)} %copy-done.5, f32[32,8,2,512]{3,0,2,1:T(8,128)S(1)} %copy_dynamic-update-slice_fusion), kind=kOutput, calls=%fused_computation.1 | convolution fusion | flops 268959744 | bytes 7340032 | tf_op jit(solution)/shard_map/jopn,omn->jopm/dot_general | solution.py:395
  89.6 0.8 copy.81
  90.5 0.2 copy.65
  90.7 0.2 fusion.3
  90.9 0.2 convolution_add_fusion.2
  91.2 13.4 %group_sums.2 = f32[32,1024]{1,0:T(8,128)S(1)} custom-call(f32[4,32,1024]{2,1,0:T(8,128)S(1)} %bitcast.175), custom_call_target="tpu_custom_call" | custom-call | tf_op jit(solution)/shard_map/group_sums/pallas_call | solution.py:318
  104.6 0.1 reshape.1232
  104.7 0.1 fusion.48
  104.8 0.1 constant_dynamic-slice_fusion.2
  104.9 0.6 fusion.18
  105.5 0.8 copy.59
  106.3 0.3 fusion.16
  106.7 0.1 copy_dynamic-update-slice_fusion.2
  106.7 3.6 %fusion.45 = f32[8,4,2,512]{3,1,2,0:T(4,128)S(1)} fusion(bf16[8,512,512,1]{2,1,3,0:T(8,128)(2,1)} %constant.56, f32[4,8,2,512]{3,0,2,1:T(4,128)S(1)} %copy_dynamic-update-slice_fusion.2), kind=kOutput, calls=%fused_computation.97 | convolution fusion | flops 33587200 | bytes 4456448 | tf_op jit(solution)/shard_map/jopn,omn->jopm/dot_general | solution.py:395
  110.3 1.2 convolution_add_fusion.4
  111.5 1.2 fusion.1
  112.8 0.1 copy.82
  112.9 0.1 fusion.26
  113.0 0.1 convolution_add_fusion.5
  113.2 7.8 %group_sums.3 = f32[4,1024]{1,0:T(4,128)S(1)} custom-call(f32[4,4,1024]{2,1,0:T(4,128)S(1)} %reshape.1235.part_ref), custom_call_target="tpu_custom_call" | custom-call | tf_op jit(solution)/shard_map/group_sums/pallas_call | solution.py:318
  121.0 0.1 constant_dynamic-slice_fusion
  121.1 0.2 multiply_subtract_fusion.2
  121.3 0.6 copy.60
  (41 shorter events, 0.3 us)
Async XLA Ops:
  0.6 74.2 %copy-start = (s32[1,8,16]{2,1,0:T(8,128)S(1)}, s32[1,8,16]{2,1,0:T(8,128)}, u32[]{:S(2)}) copy-start(s32[1,8,16]{2,1,0:T(8,128)} %param.19) | copy-start | bytes 1540
  2.0 2.5 %copy-start.1 = (f32[1024,5,256]{2,0,1:T(8,128)S(1)}, f32[1024,5,256]{2,0,1:T(8,128)}, u32[]{:S(2)}) copy-start(f32[1024,5,256]{2,0,1:T(8,128)} %param.15) | copy-start | bytes 15728644
  4.5 0.8 copy-start.2
  72.7 1.9 %copy-start.14 = (f32[16,2]{0,1:T(2,128)S(1)}, f32[16,2]{0,1:T(2,128)}, u32[]{:S(2)}) copy-start(f32[16,2]{0,1:T(2,128)} %param.22) | copy-start | bytes 388
  72.7 1.9 %copy-start.15 = (s32[1,16]{1,0:T(1,128)S(1)}, s32[1,16]{1,0:T(1,128)}, u32[]{:S(2)}) copy-start(s32[1,16]{1,0:T(1,128)} %param.21) | copy-start | bytes 196
  72.7 2.8 %copy-start.7 = (f32[8,512]{1,0:T(8,128)S(1)}, f32[8,512]{1,0:T(8,128)}, u32[]{:S(2)}) copy-start(f32[8,512]{1,0:T(8,128)} %constant.49) | copy-start | bytes 49156
  72.7 3.1 %copy-start.16 = (s32[1,128]{1,0:T(1,128)S(1)}, s32[1,128]{1,0:T(1,128)}, u32[]{:S(2)}) copy-start(s32[1,128]{1,0:T(1,128)} %param.20) | copy-start | bytes 1540
  72.8 3.3 %copy-start.13 = (s32[1,8,32]{2,1,0:T(8,128)S(1)}, s32[1,8,32]{2,1,0:T(8,128)}, u32[]{:S(2)}) copy-start(s32[1,8,32]{2,1,0:T(8,128)} %param.18) | copy-start | bytes 3076
  72.8 3.9 %copy-start.8 = (f32[8,512]{1,0:T(8,128)S(1)}, f32[8,512]{1,0:T(8,128)}, u32[]{:S(2)}) copy-start(f32[8,512]{1,0:T(8,128)} %constant.47) | copy-start | bytes 49156
  73.2 3.8 %copy-start.9 = (f32[8,512]{1,0:T(8,128)S(1)}, f32[8,512]{1,0:T(8,128)}, u32[]{:S(2)}) copy-start(f32[8,512]{1,0:T(8,128)} %constant.45) | copy-start | bytes 49156
  82.0 4.1 %copy-start.3 = (bf16[8,512,512,1]{2,1,3,0:T(8,128)(2,1)S(1)}, bf16[8,512,512,1]{2,1,3,0:T(8,128)(2,1)}, u32[]{:S(2)}) copy-start(bf16[8,512,512,1]{2,1,3,0:T(8,128)(2,1)} %constant.56) | copy-start | bytes 12582916
  86.0 2.2 %copy-start.5 = (bf16[8,512,512,1]{2,1,3,0:T(8,128)(2,1)S(1)}, bf16[8,512,512,1]{2,1,3,0:T(8,128)(2,1)}, u32[]{:S(2)}) copy-start(bf16[8,512,512,1]{2,1,3,0:T(8,128)(2,1)} %constant.57) | copy-start | bytes 12582916
  89.6 15.3 %copy-start.10 = (f32[512]{0:T(512)S(1)}, f32[512]{0:T(512)}, u32[]{:S(2)}) copy-start(f32[512]{0:T(512)} %constant.55) | copy-start | bytes 6148
  89.6 15.3 %copy-start.11 = (f32[512]{0:T(512)S(1)}, f32[512]{0:T(512)}, u32[]{:S(2)}) copy-start(f32[512]{0:T(512)} %constant.53) | copy-start | bytes 6148
  89.6 15.3 %copy-start.12 = (f32[512]{0:T(512)S(1)}, f32[512]{0:T(512)}, u32[]{:S(2)}) copy-start(f32[512]{0:T(512)} %constant.51) | copy-start | bytes 6148
  104.8 5.5 %copy-start.4 = (bf16[8,512,512,1]{2,1,3,0:T(8,128)(2,1)S(1)}, bf16[8,512,512,1]{2,1,3,0:T(8,128)(2,1)}, u32[]{:S(2)}) copy-start(bf16[8,512,512,1]{2,1,3,0:T(8,128)(2,1)} %constant.56) | copy-start | bytes 12582916
  106.7 4.8 %copy-start.6 = (bf16[8,512,512,1]{2,1,3,0:T(8,128)(2,1)S(1)}, bf16[8,512,512,1]{2,1,3,0:T(8,128)(2,1)}, u32[]{:S(2)}) copy-start(bf16[8,512,512,1]{2,1,3,0:T(8,128)(2,1)} %constant.57) | copy-start | bytes 12582916

commit v2 on v1

--- a/solution.py
+++ b/solution.py
@@ -56,7 +56,8 @@
             rows[j, center] = others[j]
         rows[3, center] = 1.0 / scale
         rows[4, center] = nodes[center] / scale
-    return rows.astype(np.float32)
+    even = np.array([0, 2, 4, 6, 0, 2, 4, 6])
+    return np.concatenate([rows, rows[:, even], rows[:, even + 1]]).astype(np.float32)
 
 
 def octant_tables():
@@ -84,81 +85,6 @@
         ]
     )
     return grid.reshape(3, 512).astype(np.float32)
-
-
-def term_kernel(block, unroll, index_ref, const_ref, point_ref, out_ref):
-    step = pl.program_id(0)
-    width = point_ref.shape[2]
-
-    @pl.when(step == 0)
-    def _():
-        def clear(i, carry):
-            out_ref[pl.ds(pl.multiple_of(i * 8, 8), 8)] = jnp.zeros((8, 8, 128), jnp.float32)
-            return carry
-
-        lax.fori_loop(0, out_ref.shape[0] // 8, clear, 0)
-
-    tau = [const_ref[j] for j in range(5)]
-    low = lax.broadcasted_iota(jnp.int32, (8, 128), 1) < 64
-
-    def basis(row):
-        row = jnp.broadcast_to(row, (8, width))
-        square = row * row
-        value = (square - tau[0]) * (square - tau[1]) * (square - tau[2])
-        return value * (row * tau[3] + tau[4])
-
-    def factors(rows, i):
-        first = basis(rows[0, i : i + 1])
-        second = basis(rows[1, i : i + 1])
-        third = basis(rows[2, i : i + 1])
-        weighted = jnp.concatenate(
-            [rows[3, i : i + 1] * first, rows[4, i : i + 1] * first], axis=0
-        ).astype(jnp.bfloat16)
-        pair = jnp.concatenate(
-            [second[b : b + 1] * third for b in range(8)], axis=0
-        ).astype(jnp.bfloat16)
-        return weighted, pair
-
-    def body(j, carry):
-        base = pl.multiple_of(j * 2 * unroll, 8)
-        rows = point_ref[:, pl.ds(base, 2 * unroll), :]
-        values = []
-        for k in range(unroll):
-            wa, pa = factors(rows, 2 * k)
-            wb, pb = factors(rows, 2 * k + 1)
-            result = lax.dot_general(
-                jnp.concatenate([wa, wb], axis=0),
-                jnp.concatenate([pa, pb], axis=0),
-                (((1,), (1,)), ((), ())),
-                preferred_element_type=jnp.float32,
-            )
-            values.append(jnp.where(low, result[0:8], pltpu.roll(result[8:16], 64, 1)))
-            values.append(jnp.where(low, pltpu.roll(result[16:24], 64, 1), result[24:32]))
-        for i, value in enumerate(values):
-            out_ref[index_ref[step * block + base + i]] += value
-        return carry
-
-    lax.fori_loop(0, block // (2 * unroll), body, 0)
-
-
-def dense_terms(points, index, rows):
-    _, count, width = points.shape
-    block = 128
-    return pl.pallas_call(
-        functools.partial(term_kernel, block, 16),
-        out_shape=jax.ShapeDtypeStruct((rows, 8, 128), jnp.float32),
-        grid_spec=pltpu.PrefetchScalarGridSpec(
-            num_scalar_prefetch=1,
-            grid=(count // block,),
-            in_specs=[
-                pl.BlockSpec((5, 8, width), lambda i, index: (0, 0, 0)),
-                pl.BlockSpec((5, block, width), lambda i, index: (0, i, 0)),
-            ],
-            out_specs=pl.BlockSpec((rows, 8, 128), lambda i, index: (0, 0, 0)),
-        ),
-        compiler_params=pltpu.CompilerParams(vmem_limit_bytes=48 * 1024 * 1024),
-        name="bin_terms",
-    )(index, jnp.asarray(basis_constants(width)), points)
 
 
 def greet(axis, targets):
@@ -189,101 +115,206 @@
     return plans
 
 
-def halving_kernel(axis, n, dense_ref, out_ref, kept, got, load_sem, send_sem, recv_sem):
+def migrate_kernel(
+    axis,
+    n,
+    unroll,
+    order_ref,
+    const_ref,
+    label_ref,
+    point_ref,
+    out_ref,
+    terms,
+    work,
+    near,
+    far,
+    near_send,
+    near_recv,
+    far_send,
+    far_recv,
+):
     me = lax.axis_index(axis)
     depth = n.bit_length() - 1
-    half = out_ref.shape[0] // 2
+    width = point_ref.shape[2]
+    rows = out_ref.shape[0]
+    half = rows // 2
+    capacity = label_ref.shape[2]
     bits = [(me // 2**k) % 2 for k in range(depth)]
     plans = halving_plan(n)
     partners = [me + 2**k * (1 - 2 * bits[k]) for k in range(depth)]
     greet(axis, partners)
-
-    def block(mask):
-        return sum(2**k * ((bits[k] + (mask >> k) % 2) % 2) for k in range(depth))
+    lane = lax.broadcasted_iota(jnp.int32, (8, 128), 1) < 64
+    upper = lax.broadcasted_iota(jnp.int32, (8, width), 0) < 4
+
+    def basis(row, kind):
+        row = jnp.broadcast_to(row, (8, width))
+        square = row * row
+        tau = [const_ref[5 * kind + j] for j in range(5)]
+        value = (square - tau[0]) * (square - tau[1]) * (square - tau[2])
+        return value * (row * tau[3] + tau[4])
+
+    def factors(spot):
+        row = [point_ref[c, pl.ds(spot, 1), :] for c in range(5)]
+        second = basis(row[1], 0)
+        third = basis(row[2], 0)
+        density = jnp.where(
+            upper, jnp.broadcast_to(row[3], (8, width)), jnp.broadcast_to(row[4], (8, width))
+        )
+        weighted = jnp.concatenate(
+            [density * basis(row[0], 1), density * basis(row[0], 2)], axis=0
+        ).astype(jnp.bfloat16)
+        pair = jnp.concatenate(
+            [second[b : b + 1] * third for b in range(8)], axis=0
+        ).astype(jnp.bfloat16)
+        return weighted, pair
+
+    def compute(mask):
+        block = sum(2**k * ((bits[k] + (mask // 2**k) % 2) % 2) for k in range(depth))
+
+        def bins(j, carry):
+            base = j * 2 * unroll
+            values = []
+            for k in range(unroll):
+                wa, pa = factors(order_ref[block * capacity + base + 2 * k])
+                wb, pb = factors(order_ref[block * capacity + base + 2 * k + 1])
+                result = lax.dot_general(
+                    jnp.concatenate([wa, wb], axis=0),
+                    jnp.concatenate([pa, pb], axis=0),
+                    (((1,), (1,)), ((), ())),
+                    preferred_element_type=jnp.float32,
+                )
+                values.append(jnp.where(lane, result[0:8], pltpu.roll(result[8:16], 64, 1)))
+                values.append(jnp.where(lane, pltpu.roll(result[16:24], 64, 1), result[24:32]))
+            for i, value in enumerate(values):
+                terms[pl.ds(base + i, 8, stride=capacity), :] = value
+            return carry
+
+        lax.fori_loop(0, capacity // (2 * unroll), bins, 0)
+        picks = (
+            lax.broadcasted_iota(jnp.int32, (rows, capacity), 0) == label_ref[block]
+        ).astype(jnp.float32).astype(jnp.bfloat16)
+        picks = jnp.concatenate([picks, picks], axis=1)
+        for pairing in range(4):
+            parts = [
+                terms[(2 * pairing + e) * capacity : (2 * pairing + e + 1) * capacity, :]
+                for e in range(2)
+            ]
+            value = jnp.concatenate(parts, axis=1)
+            high = value.astype(jnp.bfloat16)
+            low = (value - high.astype(jnp.float32)).astype(jnp.bfloat16)
+            work[mask, :, 256 * pairing : 256 * (pairing + 1)] = jnp.dot(
+                picks, jnp.concatenate([high, low], axis=0), preferred_element_type=jnp.float32
+            )
+
+    def near_copy(h, pair):
+        return pltpu.make_async_remote_copy(
+            src_ref=work.at[2 * pair + 1, pl.ds(h * half, half)],
+            dst_ref=near.at[h, pair],
+            send_sem=near_send.at[h, pair],
+            recv_sem=near_recv.at[h, pair],
+            device_id={axis: partners[0]},
+            device_id_type=pl.DeviceIdType.MESH,
+        )
 
     slots = {}
     for h in range(2):
-        for s, (bit, masks) in enumerate(plans[h]):
-            for mask in masks:
+        for s in range(1, depth):
+            for mask in plans[h][s][1]:
                 slots[(h, s, mask)] = len(slots)
-    copies = {}
-
-    def send(h, s, mask, source):
+
+    def far_copy(h, s, mask):
         slot = slots[(h, s, mask)]
-        copy = pltpu.make_async_remote_copy(
-            src_ref=source,
-            dst_ref=got.at[slot],
-            send_sem=send_sem.at[slot],
-            recv_sem=recv_sem.at[slot],
+        return pltpu.make_async_remote_copy(
+            src_ref=work.at[mask, pl.ds(h * half, half)],
+            dst_ref=far.at[slot],
+            send_sem=far_send.at[slot],
+            recv_sem=far_recv.at[slot],
             device_id={axis: partners[plans[h][s][0]]},
             device_id_type=pl.DeviceIdType.MESH,
         )
-        copy.start()
-        copies[(h, s, mask)] = copy
-
-    for j in range(n // 2):
+
+    def add(mask, h, other, target=None):
+        def step(i, carry):
+            spot = pl.ds(pl.multiple_of(h * half + i * 8, 8), 8)
+            total = work[mask, spot] + other[pl.ds(pl.multiple_of(i * 8, 8), 8)]
+            if target is None:
+                work[mask, spot] = total
+            else:
+                target[spot] = total
+            return carry
+
+        lax.fori_loop(0, half // 8, step, 0)
+
+    def exchange(i, carry):
+        pair = n // 2 - 1 - i
+
+        def one(r, carry):
+            compute(2 * pair + 1 - r)
+
+            @pl.when(r == 0)
+            def _():
+                for h in range(2):
+                    near_copy(h, pair).start()
+
+            return carry
+
+        lax.fori_loop(0, 2, one, 0)
         for h in range(2):
-            mask = plans[h][0][1][j]
-            send(h, 0, mask, dense_ref.at[block(mask), pl.ds(h * half, half)])
-    loads = {}
-    for j in range(n // 2):
-        for h in range(2):
-            mask = plans[h][0][1][j] - 1
-            load = pltpu.make_async_copy(
-                dense_ref.at[block(mask), pl.ds(h * half, half)],
-                kept.at[h, mask // 2],
-                load_sem.at[h, mask // 2],
-            )
-            load.start()
-            loads[(h, mask)] = load
-    for s in range(depth):
+            near_copy(h, pair).wait_recv()
+            add(2 * pair, h, near.at[h, pair])
+            if depth > 1:
+                for mask in plans[h][1][1]:
+
+                    @pl.when(2 * pair == mask)
+                    def _(h=h, mask=mask):
+                        far_copy(h, 1, mask).start()
+
+        return carry
+
+    lax.fori_loop(0, n // 2, exchange, 0)
+    for s in range(1, depth):
         for j in range(n >> (s + 1)):
             for h in range(2):
                 bit, masks = plans[h][s]
-                mask = masks[j]
-                goal = mask - 2**bit
-                if s == 0:
-                    loads[(h, goal)].wait()
-                copies[(h, s, mask)].wait_recv()
-                slot = slots[(h, s, mask)]
-
-                def add(i, carry, h=h, goal=goal, slot=slot):
-                    rows = pl.ds(pl.multiple_of(i * 8, 8), 8)
-                    total = kept[h, goal // 2, rows] + got[slot, rows]
-                    if goal == 0 and s == depth - 1:
-                        out_ref[pl.ds(pl.multiple_of(h * half + i * 8, 8), 8)] = total
-                    else:
-                        kept[h, goal // 2, rows] = total
-                    return carry
-
-                lax.fori_loop(0, half // 8, add, 0)
+                goal = masks[j] - 2**bit
+                far_copy(h, s, masks[j]).wait_recv()
+                last = goal == 0 and s == depth - 1
+                add(goal, h, far.at[slots[(h, s, masks[j])]], out_ref if last else None)
                 if goal and (goal >> plans[h][s + 1][0]) % 2 == 1:
-                    send(h, s + 1, goal, kept.at[h, goal // 2])
-    for copy in copies.values():
-        copy.wait_send()
-
-
-def halving_scatter(dense, axis, n, number):
-    rows = dense.shape[1]
-    tile = dense.shape[2:]
+                    far_copy(h, s + 1, goal).start()
+    for h in range(2):
+        for pair in range(n // 2):
+            near_copy(h, pair).wait_send()
+    for h, s, mask in slots:
+        far_copy(h, s, mask).wait_send()
+
+
+def migrate(points, order, labels, axis, n, rows, number):
+    width = points.shape[2]
+    capacity = labels.shape[1]
     half = rows // 2
+    later = 2 * (n - 1 - n // 2)
+    vmem = pl.BlockSpec(memory_space=pltpu.VMEM)
     return pl.pallas_call(
-        functools.partial(halving_kernel, axis, n),
-        out_shape=jax.ShapeDtypeStruct((rows,) + tile, jnp.float32),
-        in_specs=[pl.BlockSpec(memory_space=pl.ANY)],
-        out_specs=pl.BlockSpec(memory_space=pltpu.VMEM),
+        functools.partial(migrate_kernel, axis, n, 16),
+        out_shape=jax.ShapeDtypeStruct((rows, 1024), jnp.float32),
+        in_specs=[pl.BlockSpec(memory_space=pltpu.SMEM), vmem, vmem, vmem],
+        out_specs=vmem,
         scratch_shapes=[
-            pltpu.VMEM((2, n // 2, half) + tile, jnp.float32),
-            pltpu.VMEM((2 * (n - 1), half) + tile, jnp.float32),
+            pltpu.VMEM((8 * capacity, 128), jnp.float32),
+            pltpu.VMEM((n, rows, 1024), jnp.float32),
+            pltpu.VMEM((2, n // 2, half, 1024), jnp.float32),
+            pltpu.VMEM((later, half, 1024), jnp.float32),
             pltpu.SemaphoreType.DMA((2, n // 2)),
-            pltpu.SemaphoreType.DMA((2 * (n - 1),)),
-            pltpu.SemaphoreType.DMA((2 * (n - 1),)),
+            pltpu.SemaphoreType.DMA((2, n // 2)),
+            pltpu.SemaphoreType.DMA((later,)),
+            pltpu.SemaphoreType.DMA((later,)),
         ],
         compiler_params=pltpu.CompilerParams(
-            collective_id=number, has_side_effects=True, vmem_limit_bytes=48 * 1024 * 1024
+            collective_id=number, has_side_effects=True, vmem_limit_bytes=56 * 1024 * 1024
         ),
-        name="segment_sums",
-    )(dense)
+        name="migrate",
+    )(order, jnp.asarray(basis_constants(width)), labels[:, None, :], points)
 
 
 def direct_kernel(axis, n, part_ref, out_ref, got, send_sem, recv_sem):
@@ -367,8 +398,8 @@
 
 
 def split(values):
-    high = values.astype(jnp.bfloat16)
-    return high, (values - high.astype(jnp.float32)).astype(jnp.bfloat16)
+    high = lax.reduce_precision(values, 8, 7)
+    return high.astype(jnp.bfloat16), (values - high).astype(jnp.bfloat16)
 
 
 def level_partial(children, slots, parent_dirs, kappa, matrices):
@@ -413,12 +444,24 @@
     groups = lax.axis_size("grp")
     group_rank = lax.axis_index("grp")
     leaf_count = leaf_slots.shape[2] * 8
-    index = bin_plan[:, 0] * leaf_count + bin_leaf
-    dense = dense_terms(jnp.transpose(bin_points, (1, 0, 2)), index, peers * leaf_count)
-    own = halving_scatter(dense.reshape(peers, leaf_count, 8, 128), "sfc", peers, 0)
-    leaves = jnp.transpose(own.reshape(leaf_count, 8, 2, 64), (0, 2, 1, 3)).reshape(
-        leaf_count, 2, 512
-    )
+    count = bin_points.shape[0]
+    capacity = count // 8
+    target = bin_plan[:, 0]
+    number = jnp.arange(count, dtype=jnp.int32)
+    ahead = (target[:, None] == target[None, :]) & (number[None, :] < number[:, None])
+    position = target * capacity + jnp.sum(ahead.astype(jnp.int32), axis=1)
+    taken = jnp.arange(peers * capacity, dtype=jnp.int32)[:, None] == position[None, :]
+    order = jnp.sum(jnp.where(taken, number[None, :], 0), axis=1)
+    labels = jnp.sum(jnp.where(taken, bin_leaf[None, :] + 1, 0), axis=1) - 1
+    leaves = migrate(
+        jnp.transpose(bin_points, (1, 0, 2)),
+        order,
+        labels.reshape(peers, capacity),
+        "sfc",
+        peers,
+        leaf_count,
+        0,
+    ).reshape(leaf_count, 2, 512)
     exact = child_matrices()
     rounded = exact.astype(ml_dtypes.bfloat16)
     rest = (exact - rounded.astype(np.float64)).astype(ml_dtypes.bfloat16)

time: 122 us -> 101 us (0.83)
  Pallas kernels: 88.6 us -> 71.4 us
  local copies, waits for them, and re-layouts: 11.9 us -> 8.66 us
  matrix products: 13.9 us -> 11.5 us
  other arithmetic: 6.37 us -> 7.72 us
    pallas_call x2 -> x1, Pallas kernels: 67.4 us -> 51.3 us  [migrate(): pl.pallas_call(functools.partial(migrate_kernel, axis, n, 16), out_shape=...]
    unnamed x41 -> x38, local copies, waits for them, and re-layouts: 7.43 us -> 2.86 us
    reduce_sum x0 -> x2, other arithmetic: none -> 3.15 us  [the longest x1 1.86 us: per_device(): labels = jnp.sum(jnp.where(taken, bin_leaf[None, :] + 1, 0), axis=1) - 1]
    dot_general x6, matrix products: 12.5 us -> 10.1 us  [level_partial(): jnp.einsum('jopn,omn->jopm', value, matrix, preferred_element_type=jnp.fl...]
    another operation x4 -> x5, other arithmetic: 0.94 us -> 3.06 us  [rotate(): jnp.stack([real_part * cosine - imag_part * sine, real_part * sine + imag...]
    reshape x0 -> x1, local copies, waits for them, and re-layouts: none -> 2.11 us  [per_device(): leaves = migrate(jnp.transpose(bin_points, (1, 0, 2)), order, labels.resh...]
    add x2 -> x1, other arithmetic: 2.7 us -> 0.71 us  [per_device(): position = target * capacity + jnp.sum(ahead.astype(jnp.int32), axis=1)]
    cos x1 -> x0, other arithmetic: 1.83 us -> none  [level_partial(): turned = rotate(children, jnp.cos(angle), jnp.sin(angle))]
where the time goes in v2:
time: 101 us; the launch traced here: 100 us
  Pallas kernels  71.4 us (71%)
  matrix products  11.5 us (11%)
  local copies, waits for them, and re-layouts  8.66 us (9%)
  other arithmetic  7.72 us (8%)
  between operations  1.02 us (1%)
    pallas_call x1, Pallas kernels, migrate(): pl.pallas_call(functools.partial(migrate_kernel, axis, n, 16), out_shape=...  51.3 us
    pallas_call x2, Pallas kernels, direct_scatter(): pl.pallas_call(functools.partial(direct_kernel, axis, n), out_shape=jax.S...  20.1 us
    dot_general x6, matrix products, level_partial(): jnp.einsum('jopn,omn->jopm', value, matrix, preferred_element_type=jnp.fl...  10.1 us
    another operation x5, other arithmetic, rotate(): jnp.stack([real_part * cosine - imag_part * sine, real_part * sine + imag...  3.06 us
    unnamed x38, local copies, waits for them, and re-layouts  2.86 us
    reshape x1, local copies, waits for them, and re-layouts, per_device(): leaves = migrate(jnp.transpose(bin_points, (1, 0, 2)), order, labels.resh...  2.11 us

profile of v2, /device:TPU:0, one launch (start us, length us, event | category | flops | bytes accessed | tf_op | source)
XLA Modules:
  0.0 100.3 jit_solution(8986713558230790344)
XLA Ops:
  0.6 0.0 copy-start
  0.6 1.3 %convert_reduce_fusion = s32[1024]{0:T(1024)S(1)} fusion(s32[1024]{0:T(1024)} %bitcast.263), kind=kLoop, calls=%fused_computation.2 | loop fusion | flops 5241856 | bytes 8192 | tf_op jit(solution)/shard_map/reduce_sum | solution.py:452
  1.9 0.7 multiply_add_fusion.2
  2.6 1.9 %select_reduce_fusion = (s32[1024]{0:T(1024)S(1)}, s32[1024]{0:T(1024)}) fusion(s32[1024]{0:T(1024)S(1)} %get-tuple-element.41, s32[1024]{0:T(1024)S(1)} %get-tuple-element.40), kind=kLoop, calls=%fused_computation | loop fusion | flops 5240832 | bytes 16384 | tf_op jit(solution)/shard_map/reduce_sum | solution.py:455
  4.5 0.6 broadcast_add_fusion
  5.1 0.0 copy-start.7
  5.1 0.0 copy-start.8
  5.1 51.3 %migrate.1 = f32[256,1024]{1,0:T(8,128)} custom-call(s32[1024]{0:T(1024)} %get-tuple-element.13.order_ref, f32[15,8,256]{2,1,0:T(8,128)} %constant.39.clone.const_ref, s32[8,1,128]{2,1,0:T(1,128)} %bitcast.261, f32[5,1024,256]{2,1,0:T(8,128)} %bitcast.258), custom_call_target="tpu_custom_call" | custom-call | tf_op jit(solution)/shard_map/migrate/pallas_call | solution.py:298
  56.4 2.1 %reshape.1241 = f32[256,2,512]{2,1,0:T(2,128)S(1)} reshape(f32[256,1024]{1,0:T(8,128)} %migrate.1) | data formatting | bytes 2097152 | tf_op jit(solution)/shard_map/reshape | solution.py:464
  58.5 0.0 copy-start.5
  58.6 0.8 fusion.59
  59.4 0.1 cosine_multiply_fusion
  59.4 0.2 fusion.46
  59.6 0.1 copy.45
  59.7 0.2 eq.96
  59.9 0.1 fusion.24
  60.0 0.1 reshape.1242
  60.2 0.1 mul.507
  60.2 0.1 mul.513
  60.3 0.1 mul.519
  60.5 2.1 %fusion.20 = (f32[32,8,1,512]{3,1,0,2:T(8,128)S(1)}, f32[32,8,1,512]{3,1,0,2:T(8,128)S(1)}) fusion(f32[256,1,512]{2,1,0:T(1,128)S(1)} %get-tuple-element.20, f32[256,1,512]{2,1,0:T(1,128)S(1)} %get-tuple-element.19, f32[8,512]{1,0:T(8,128)S(1)} %copy-done.8, f32[256]{0:T(256)S(1)} %mul.519, f32[8,512]{1,0:T(8,128)S(1)} %copy-done.7, f32[256]{0:T(256)S(1)} %mul.513, ...), kind=kLoop, calls=%fused_computation.37 | loop fusion | flops 1572864 | bytes 2149376 | tf_op jit(solution)/shard_map/stack | solution.py:369
  62.6 0.3 copy_dynamic-update-slice_fusion.1
  62.9 0.3 copy_dynamic-update-slice_fusion
  63.2 1.4 %fusion.21 = f32[8,32,2,512]{3,1,2,0:T(8,128)S(1)} fusion(bf16[8,512,512,1]{2,1,3,0:T(8,128)(2,1)S(1)} %copy-done.1, f32[32,8,2,512]{3,0,2,1:T(8,128)S(1)} %copy_dynamic-update-slice_fusion), kind=kOutput, calls=%fused_computation.40 | convolution fusion | flops 268959744 | bytes 6291456 | tf_op jit(solution)/shard_map/jopn,omn->jopm/dot_general | solution.py:426
  64.6 0.0 copy-start.3
  64.6 1.4 %convolution_add_fusion.1 = f32[8,32,2,512]{3,1,2,0:T(8,128)S(1)} fusion(f32[8,32,2,512]{3,1,2,0:T(8,128)S(1)} %fusion.21, bf16[8,512,512,1]{2,1,3,0:T(8,128)(2,1)S(1)} %copy-done.1, f32[32,8,2,512]{3,0,2,1:T(8,128)S(1)} %copy_dynamic-update-slice_fusion), kind=kOutput, calls=%fused_computation.12 | convolution fusion | flops 269484032 | bytes 7340032 | tf_op jit(solution)/shard_map/jopn,omn->jopm/dot_general | solution.py:426
  66.0 0.8 copy-done.3
  66.8 1.4 %fusion.1 = f32[32,8,2,512]{3,0,2,1:T(8,128)S(1)} fusion(f32[8,32,2,512]{3,1,2,0:T(8,128)S(1)} %convolution_add_fusion.1, bf16[8,512,512,1]{2,1,3,0:T(8,128)(2,1)S(1)} %copy-done.3, f32[32,8,2,512]{3,0,2,1:T(8,128)S(1)} %copy_dynamic-update-slice_fusion), kind=kOutput, calls=%fused_computation.11 | convolution fusion | flops 269221888 | bytes 7340032 | tf_op jit(solution)/shard_map/jopn,omn->jopm/dot_general | solution.py:426
  68.2 0.0 copy-start.9
  68.2 0.0 copy-start.10
  68.2 0.0 copy-start.11
  68.2 0.8 copy.87
  69.0 0.2 copy.67
  69.3 0.2 fusion.7
  69.5 0.3 convolution_add_fusion.2
  69.8 12.3 %group_sums.2 = f32[32,1024]{1,0:T(8,128)S(1)} custom-call(f32[4,32,1024]{2,1,0:T(8,128)S(1)} %bitcast.254), custom_call_target="tpu_custom_call" | custom-call | tf_op jit(solution)/shard_map/group_sums/pallas_call | solution.py:349
  82.0 0.1 reshape.1245
  82.2 0.1 fusion.60
  82.3 0.1 constant_dynamic-slice_fusion
  82.4 0.1 copy.53
  82.4 0.1 eq.104
  82.5 0.2 fusion.50
  82.7 0.1 fusion.49
  82.9 0.1 reshape.1246
  82.9 0.1 mul.548
  83.0 0.1 mul.554
  83.1 0.1 mul.560
  83.2 0.1 constant_dynamic-slice_fusion.1
  83.3 0.6 fusion.40
  83.9 0.3 fusion.38
  84.3 0.1 copy_dynamic-update-slice_fusion.2
  84.4 3.6 %fusion.48 = f32[8,4,2,512]{3,1,2,0:T(4,128)S(1)} fusion(bf16[8,512,512,1]{2,1,3,0:T(8,128)(2,1)} %constant.60, f32[4,8,2,512]{3,0,2,1:T(4,128)S(1)} %copy_dynamic-update-slice_fusion.2), kind=kOutput, calls=%fused_computation.81 | convolution fusion | flops 33619968 | bytes 4456448 | tf_op jit(solution)/shard_map/jopn,omn->jopm/dot_general | solution.py:426
  87.9 0.0 copy-done.2
  87.9 1.2 %convolution_add_fusion.4 = f32[8,4,2,512]{3,1,2,0:T(4,128)S(1)} fusion(f32[8,4,2,512]{3,1,2,0:T(4,128)S(1)} %fusion.48, bf16[8,512,512,1]{2,1,3,0:T(8,128)(2,1)S(1)} %copy-done.2, f32[4,8,2,512]{3,0,2,1:T(4,128)S(1)} %copy_dynamic-update-slice_fusion.2), kind=kOutput, calls=%fused_computation.16 | convolution fusion | flops 33685504 | bytes 4587520 | tf_op jit(solution)/shard_map/jopn,omn->jopm/dot_general | solution.py:426
  89.2 0.0 copy-done.4
  89.2 1.2 %fusion.2 = f32[4,8,2,512]{3,0,2,1:T(4,128)S(1)} fusion(f32[8,4,2,512]{3,1,2,0:T(4,128)S(1)} %convolution_add_fusion.4, bf16[8,512,512,1]{2,1,3,0:T(8,128)(2,1)S(1)} %copy-done.4, f32[4,8,2,512]{3,0,2,1:T(4,128)S(1)} %copy_dynamic-update-slice_fusion.2), kind=kOutput, calls=%fused_computation.15 | convolution fusion | flops 33652736 | bytes 4587520 | tf_op jit(solution)/shard_map/jopn,omn->jopm/dot_general | solution.py:426
  90.4 0.1 copy.88
  90.5 0.1 fusion.27
  90.6 0.1 convolution_add_fusion.5
  90.8 7.8 %group_sums.3 = f32[4,1024]{1,0:T(4,128)S(1)} custom-call(f32[4,4,1024]{2,1,0:T(4,128)S(1)} %reshape.1248.part_ref), custom_call_target="tpu_custom_call" | custom-call | tf_op jit(solution)/shard_map/group_sums/pallas_call | solution.py:349
  98.6 0.1 constant_dynamic-slice_fusion.2
  98.7 0.2 multiply_subtract_fusion.1
  98.9 0.6 copy.60
  99.5 0.8 copy.59
  (30 shorter events, 0.2 us)
Async XLA Ops:
  0.6 81.6 %copy-start = (s32[1,8,16]{2,1,0:T(8,128)S(1)}, s32[1,8,16]{2,1,0:T(8,128)}, u32[]{:S(2)}) copy-start(s32[1,8,16]{2,1,0:T(8,128)} %param.19) | copy-start | bytes 1540
  5.1 54.3 %copy-start.13 = (f32[16,2]{0,1:T(2,128)S(1)}, f32[16,2]{0,1:T(2,128)}, u32[]{:S(2)}) copy-start(f32[16,2]{0,1:T(2,128)} %param.22) | copy-start | bytes 388
  5.1 54.3 %copy-start.14 = (s32[1,128]{1,0:T(1,128)S(1)}, s32[1,128]{1,0:T(1,128)}, u32[]{:S(2)}) copy-start(s32[1,128]{1,0:T(1,128)} %param.20) | copy-start | bytes 1540
  5.1 54.5 %copy-start.12 = (s32[1,8,32]{2,1,0:T(8,128)S(1)}, s32[1,8,32]{2,1,0:T(8,128)}, u32[]{:S(2)}) copy-start(s32[1,8,32]{2,1,0:T(8,128)} %param.18) | copy-start | bytes 3076
  5.1 55.3 %copy-start.6 = (f32[8,512]{1,0:T(8,128)S(1)}, f32[8,512]{1,0:T(8,128)}, u32[]{:S(2)}) copy-start(f32[8,512]{1,0:T(8,128)} %constant.49) | copy-start | bytes 49156
  5.1 55.3 %copy-start.7 = (f32[8,512]{1,0:T(8,128)S(1)}, f32[8,512]{1,0:T(8,128)}, u32[]{:S(2)}) copy-start(f32[8,512]{1,0:T(8,128)} %constant.51) | copy-start | bytes 49156
  5.1 55.3 %copy-start.8 = (f32[8,512]{1,0:T(8,128)S(1)}, f32[8,512]{1,0:T(8,128)}, u32[]{:S(2)}) copy-start(f32[8,512]{1,0:T(8,128)} %constant.53) | copy-start | bytes 49156
  58.5 6.1 %copy-start.5 = (f32[256,2,512]{2,1,0:T(2,128)}, f32[256,2,512]{2,1,0:T(2,128)S(1)}, u32[]{:S(2)}) copy-start(f32[256,2,512]{2,1,0:T(2,128)S(1)} %reshape.1241) | copy-start | bytes 3145732
  60.5 2.8 %copy-start.1 = (bf16[8,512,512,1]{2,1,3,0:T(8,128)(2,1)S(1)}, bf16[8,512,512,1]{2,1,3,0:T(8,128)(2,1)}, u32[]{:S(2)}) copy-start(bf16[8,512,512,1]{2,1,3,0:T(8,128)(2,1)} %constant.60) | copy-start | bytes 12582916
  64.6 2.2 %copy-start.3 = (bf16[8,512,512,1]{2,1,3,0:T(8,128)(2,1)S(1)}, bf16[8,512,512,1]{2,1,3,0:T(8,128)(2,1)}, u32[]{:S(2)}) copy-start(bf16[8,512,512,1]{2,1,3,0:T(8,128)(2,1)} %constant.61) | copy-start | bytes 12582916
  68.2 14.4 %copy-start.15 = (s32[1,16]{1,0:T(1,128)S(1)}, s32[1,16]{1,0:T(1,128)}, u32[]{:S(2)}) copy-start(s32[1,16]{1,0:T(1,128)} %param.21) | copy-start | bytes 196
  68.2 15.1 %copy-start.9 = (f32[512]{0:T(512)S(1)}, f32[512]{0:T(512)}, u32[]{:S(2)}) copy-start(f32[512]{0:T(512)} %constant.55) | copy-start | bytes 6148
  68.2 15.1 %copy-start.10 = (f32[512]{0:T(512)S(1)}, f32[512]{0:T(512)}, u32[]{:S(2)}) copy-start(f32[512]{0:T(512)} %constant.57) | copy-start | bytes 6148
  68.2 15.1 %copy-start.11 = (f32[512]{0:T(512)S(1)}, f32[512]{0:T(512)}, u32[]{:S(2)}) copy-start(f32[512]{0:T(512)} %constant.59) | copy-start | bytes 6148
  83.2 4.7 %copy-start.2 = (bf16[8,512,512,1]{2,1,3,0:T(8,128)(2,1)S(1)}, bf16[8,512,512,1]{2,1,3,0:T(8,128)(2,1)}, u32[]{:S(2)}) copy-start(bf16[8,512,512,1]{2,1,3,0:T(8,128)(2,1)} %constant.60) | copy-start | bytes 12582916
  84.4 4.8 %copy-start.4 = (bf16[8,512,512,1]{2,1,3,0:T(8,128)(2,1)S(1)}, bf16[8,512,512,1]{2,1,3,0:T(8,128)(2,1)}, u32[]{:S(2)}) copy-start(bf16[8,512,512,1]{2,1,3,0:T(8,128)(2,1)} %constant.61) | copy-start | bytes 12582916

commit v3 on v2

--- a/solution.py
+++ b/solution.py
@@ -423,11 +423,8 @@
     angle = kappa * angle.reshape(count, 512)
     turned = rotate(children, jnp.cos(angle), jnp.sin(angle))
     moved = sum(
-        jnp.einsum("jopn,omn->jopm", value, matrix, preferred_element_type=jnp.float32)
-        for value, matrix in zip(
-            split(turned.reshape(count // 8, 8, 2, 512)) + split(turned.reshape(count // 8, 8, 2, 512))[:1],
-            (matrices[0], matrices[0], matrices[1]),
-        )
+        jnp.einsum("jopn,omn->jopm", value, matrices, preferred_element_type=jnp.float32)
+        for value in split(turned.reshape(count // 8, 8, 2, 512))
     )
     picks = match.astype(jnp.bfloat16)
     high, low = split(moved.reshape(count, 1024))
@@ -462,10 +459,7 @@
         leaf_count,
         0,
     ).reshape(leaf_count, 2, 512)
-    exact = child_matrices()
-    rounded = exact.astype(ml_dtypes.bfloat16)
-    rest = (exact - rounded.astype(np.float64)).astype(ml_dtypes.bfloat16)
-    matrices = (jnp.asarray(rounded), jnp.asarray(rest))
+    matrices = jnp.asarray(child_matrices().astype(ml_dtypes.bfloat16))
     directions = cone_vectors(cone_angles)
     parent_dirs = look_up(directions, parent_cone[0])
     upper_dirs = look_up(directions, box_cone[0])

time: 101 us -> 97 us (0.960)
  matrix products: 11.5 us -> 8.88 us
    dot_general x6 -> x4, matrix products: 10.1 us -> 7.49 us  [level_partial(): jnp.einsum('jopn,omn->jopm', value, matrices, preferred_element_type=jnp....]
    unnamed x38 -> x34, local copies, waits for them, and re-layouts: 2.86 us -> 2.04 us
where the time goes in v3:
time: 97 us; the launch traced here: 96.8 us
  Pallas kernels  71.4 us (74%)
  matrix products  8.88 us (9%)
  local copies, waits for them, and re-layouts  7.84 us (8%)
  other arithmetic  7.72 us (8%)
  between operations  0.99 us (1%)
    pallas_call x1, Pallas kernels, migrate(): pl.pallas_call(functools.partial(migrate_kernel, axis, n, 16), out_shape=...  51.3 us
    pallas_call x2, Pallas kernels, direct_scatter(): pl.pallas_call(functools.partial(direct_kernel, axis, n), out_shape=jax.S...  20.1 us
    dot_general x4, matrix products, level_partial(): jnp.einsum('jopn,omn->jopm', value, matrices, preferred_element_type=jnp....  7.49 us
    another operation x5, other arithmetic, rotate(): jnp.stack([real_part * cosine - imag_part * sine, real_part * sine + imag...  3.06 us
    reshape x1, local copies, waits for them, and re-layouts, per_device(): leaves = migrate(jnp.transpose(bin_points, (1, 0, 2)), order, labels.resh...  2.11 us
    unnamed x34, local copies, waits for them, and re-layouts  2.04 us

profile of v3, /device:TPU:0, one launch (start us, length us, event | category | flops | bytes accessed | tf_op | source)
XLA Modules:
  0.0 96.8 jit_solution(2833227168670994316)
XLA Ops:
  0.6 0.0 copy-start
  0.6 1.3 %convert_reduce_fusion = s32[1024]{0:T(1024)S(1)} fusion(s32[1024]{0:T(1024)} %bitcast.258), kind=kLoop, calls=%fused_computation.2 | loop fusion | flops 5241856 | bytes 8192 | tf_op jit(solution)/shard_map/reduce_sum | solution.py:449
  1.9 0.7 multiply_add_fusion.2
  2.6 1.9 %select_reduce_fusion = (s32[1024]{0:T(1024)S(1)}, s32[1024]{0:T(1024)}) fusion(s32[1024]{0:T(1024)S(1)} %get-tuple-element.41, s32[1024]{0:T(1024)S(1)} %get-tuple-element.40), kind=kLoop, calls=%fused_computation | loop fusion | flops 5240832 | bytes 16384 | tf_op jit(solution)/shard_map/reduce_sum | solution.py:452
  4.5 0.6 broadcast_add_fusion
  5.1 0.0 copy-start.5
  5.1 0.0 copy-start.6
  5.1 51.3 %migrate.1 = f32[256,1024]{1,0:T(8,128)} custom-call(s32[1024]{0:T(1024)} %get-tuple-element.13.order_ref, f32[15,8,256]{2,1,0:T(8,128)} %constant.37.clone.const_ref, s32[8,1,128]{2,1,0:T(1,128)} %bitcast.256, f32[5,1024,256]{2,1,0:T(8,128)} %bitcast.253), custom_call_target="tpu_custom_call" | custom-call | tf_op jit(solution)/shard_map/migrate/pallas_call | solution.py:298
  56.4 2.1 %reshape.1239 = f32[256,2,512]{2,1,0:T(2,128)S(1)} reshape(f32[256,1024]{1,0:T(8,128)} %migrate.1) | data formatting | bytes 2097152 | tf_op jit(solution)/shard_map/reshape | solution.py:461
  58.5 0.0 copy-start.3
  58.6 0.8 fusion.59
  59.4 0.0 copy-done.11
  59.4 0.1 cosine_multiply_fusion
  59.5 0.2 fusion.46
  59.6 0.1 copy.44
  59.7 0.2 eq.96
  59.9 0.1 fusion.24
  60.0 0.1 reshape.1240
  60.2 0.1 mul.507
  60.2 0.1 mul.513
  60.3 0.1 mul.519
  60.5 0.0 copy-start.1
  60.5 2.1 %fusion.20 = (f32[32,8,1,512]{3,1,0,2:T(8,128)S(1)}, f32[32,8,1,512]{3,1,0,2:T(8,128)S(1)}) fusion(f32[256,1,512]{2,1,0:T(1,128)S(1)} %get-tuple-element.20, f32[256,1,512]{2,1,0:T(1,128)S(1)} %get-tuple-element.19, f32[8,512]{1,0:T(8,128)S(1)} %copy-done.6, f32[256]{0:T(256)S(1)} %mul.519, f32[8,512]{1,0:T(8,128)S(1)} %copy-done.5, f32[256]{0:T(256)S(1)} %mul.513, ...), kind=kLoop, calls=%fused_computation.35 | loop fusion | flops 1572864 | bytes 2149376 | tf_op jit(solution)/shard_map/stack | solution.py:369
  62.6 0.3 copy_dynamic-update-slice_fusion.1
  62.9 0.3 copy_dynamic-update-slice_fusion
  63.2 0.0 copy-done.1
  63.2 1.4 %fusion.21 = f32[8,32,2,512]{3,1,2,0:T(8,128)S(1)} fusion(bf16[8,512,512,1]{2,1,3,0:T(8,128)(2,1)S(1)} %copy-done.1, f32[32,8,2,512]{3,0,2,1:T(8,128)S(1)} %copy_dynamic-update-slice_fusion), kind=kOutput, calls=%fused_computation.38 | convolution fusion | flops 268959744 | bytes 6291456 | tf_op jit(solution)/shard_map/jopn,omn->jopm/dot_general | solution.py:426
  64.6 1.4 %fusion.1 = f32[32,8,2,512]{3,0,2,1:T(8,128)S(1)} fusion(f32[8,32,2,512]{3,1,2,0:T(8,128)S(1)} %fusion.21, bf16[8,512,512,1]{2,1,3,0:T(8,128)(2,1)S(1)} %copy-done.1, f32[32,8,2,512]{3,0,2,1:T(8,128)S(1)} %copy_dynamic-update-slice_fusion), kind=kOutput, calls=%fused_computation.11 | convolution fusion | flops 269484032 | bytes 7340032 | tf_op jit(solution)/shard_map/jopn,omn->jopm/dot_general | solution.py:426
  66.0 0.0 copy-start.13
  66.0 0.0 copy-start.7
  66.0 0.0 copy-start.8
  66.0 0.0 copy-start.9
  66.0 0.8 copy.85
  66.9 0.2 copy.65
  67.1 0.2 fusion.7
  67.3 0.3 convolution_add_fusion.1
  67.6 12.3 %group_sums.2 = f32[32,1024]{1,0:T(8,128)S(1)} custom-call(f32[4,32,1024]{2,1,0:T(8,128)S(1)} %bitcast.249), custom_call_target="tpu_custom_call" | custom-call | tf_op jit(solution)/shard_map/group_sums/pallas_call | solution.py:349
  79.9 0.1 reshape.1243
  80.0 0.1 fusion.60
  80.1 0.1 constant_dynamic-slice_fusion
  80.2 0.1 copy.52
  80.3 0.1 eq.104
  80.3 0.2 fusion.50
  80.5 0.1 fusion.49
  80.7 0.1 reshape.1244
  80.8 0.1 mul.548
  80.8 0.1 mul.554
  80.9 0.1 mul.560
  81.0 0.1 constant_dynamic-slice_fusion.1
  81.1 0.0 copy-done.8
  81.1 0.6 fusion.40
  81.7 0.3 fusion.38
  82.1 0.1 copy_dynamic-update-slice_fusion.2
  82.2 3.5 %fusion.47 = f32[8,4,2,512]{3,1,2,0:T(4,128)S(1)} fusion(bf16[8,512,512,1]{2,1,3,0:T(8,128)(2,1)} %constant.57, f32[4,8,2,512]{3,0,2,1:T(4,128)S(1)} %copy_dynamic-update-slice_fusion.2), kind=kOutput, calls=%fused_computation.78 | convolution fusion | flops 33619968 | bytes 4456448 | tf_op jit(solution)/shard_map/jopn,omn->jopm/dot_general | solution.py:426
  85.7 0.0 copy-done.2
  85.7 1.2 %fusion.2 = f32[4,8,2,512]{3,0,2,1:T(4,128)S(1)} fusion(f32[8,4,2,512]{3,1,2,0:T(4,128)S(1)} %fusion.47, bf16[8,512,512,1]{2,1,3,0:T(8,128)(2,1)S(1)} %copy-done.2, f32[4,8,2,512]{3,0,2,1:T(4,128)S(1)} %copy_dynamic-update-slice_fusion.2), kind=kOutput, calls=%fused_computation.14 | convolution fusion | flops 33685504 | bytes 4587520 | tf_op jit(solution)/shard_map/jopn,omn->jopm/dot_general | solution.py:426
  86.9 0.1 copy.86
  87.0 0.1 fusion.27
  87.2 0.1 convolution_add_fusion.3
  87.3 7.8 %group_sums.3 = f32[4,1024]{1,0:T(4,128)S(1)} custom-call(f32[4,4,1024]{2,1,0:T(4,128)S(1)} %reshape.1246.part_ref), custom_call_target="tpu_custom_call" | custom-call | tf_op jit(solution)/shard_map/group_sums/pallas_call | solution.py:349
  95.2 0.1 constant_dynamic-slice_fusion.2
  95.2 0.2 multiply_subtract_fusion.1
  95.4 0.6 copy.59
  96.0 0.8 copy.58
  (24 shorter events, 0.2 us)
Async XLA Ops:
  0.6 79.5 %copy-start = (s32[1,8,16]{2,1,0:T(8,128)S(1)}, s32[1,8,16]{2,1,0:T(8,128)}, u32[]{:S(2)}) copy-start(s32[1,8,16]{2,1,0:T(8,128)} %param.18) | copy-start | bytes 1540
  5.1 54.3 %copy-start.11 = (f32[16,2]{0,1:T(2,128)S(1)}, f32[16,2]{0,1:T(2,128)}, u32[]{:S(2)}) copy-start(f32[16,2]{0,1:T(2,128)} %param.21) | copy-start | bytes 388
  5.1 54.3 %copy-start.12 = (s32[1,128]{1,0:T(1,128)S(1)}, s32[1,128]{1,0:T(1,128)}, u32[]{:S(2)}) copy-start(s32[1,128]{1,0:T(1,128)} %param.19) | copy-start | bytes 1540
  5.1 54.5 %copy-start.10 = (s32[1,8,32]{2,1,0:T(8,128)S(1)}, s32[1,8,32]{2,1,0:T(8,128)}, u32[]{:S(2)}) copy-start(s32[1,8,32]{2,1,0:T(8,128)} %param.17) | copy-start | bytes 3076
  5.1 55.3 %copy-start.4 = (f32[8,512]{1,0:T(8,128)S(1)}, f32[8,512]{1,0:T(8,128)}, u32[]{:S(2)}) copy-start(f32[8,512]{1,0:T(8,128)} %constant.46) | copy-start | bytes 49156
  5.1 55.3 %copy-start.5 = (f32[8,512]{1,0:T(8,128)S(1)}, f32[8,512]{1,0:T(8,128)}, u32[]{:S(2)}) copy-start(f32[8,512]{1,0:T(8,128)} %constant.48) | copy-start | bytes 49156
  5.1 55.3 %copy-start.6 = (f32[8,512]{1,0:T(8,128)S(1)}, f32[8,512]{1,0:T(8,128)}, u32[]{:S(2)}) copy-start(f32[8,512]{1,0:T(8,128)} %constant.50) | copy-start | bytes 49156
  58.5 6.1 %copy-start.3 = (f32[256,2,512]{2,1,0:T(2,128)}, f32[256,2,512]{2,1,0:T(2,128)S(1)}, u32[]{:S(2)}) copy-start(f32[256,2,512]{2,1,0:T(2,128)S(1)} %reshape.1239) | copy-start | bytes 3145732
  60.5 2.8 %copy-start.1 = (bf16[8,512,512,1]{2,1,3,0:T(8,128)(2,1)S(1)}, bf16[8,512,512,1]{2,1,3,0:T(8,128)(2,1)}, u32[]{:S(2)}) copy-start(bf16[8,512,512,1]{2,1,3,0:T(8,128)(2,1)} %constant.57) | copy-start | bytes 12582916
  66.0 14.3 %copy-start.13 = (s32[1,16]{1,0:T(1,128)S(1)}, s32[1,16]{1,0:T(1,128)}, u32[]{:S(2)}) copy-start(s32[1,16]{1,0:T(1,128)} %param.20) | copy-start | bytes 196
  66.0 15.1 %copy-start.7 = (f32[512]{0:T(512)S(1)}, f32[512]{0:T(512)}, u32[]{:S(2)}) copy-start(f32[512]{0:T(512)} %constant.52) | copy-start | bytes 6148
  66.0 15.1 %copy-start.8 = (f32[512]{0:T(512)S(1)}, f32[512]{0:T(512)}, u32[]{:S(2)}) copy-start(f32[512]{0:T(512)} %constant.54) | copy-start | bytes 6148
  66.0 15.1 %copy-start.9 = (f32[512]{0:T(512)S(1)}, f32[512]{0:T(512)}, u32[]{:S(2)}) copy-start(f32[512]{0:T(512)} %constant.56) | copy-start | bytes 6148
  81.0 4.7 %copy-start.2 = (bf16[8,512,512,1]{2,1,3,0:T(8,128)(2,1)S(1)}, bf16[8,512,512,1]{2,1,3,0:T(8,128)(2,1)}, u32[]{:S(2)}) copy-start(bf16[8,512,512,1]{2,1,3,0:T(8,128)(2,1)} %constant.57) | copy-start | bytes 12582916
